TPU v7x, 32 devices: a whole 2x2x4 slice. The times are simulated.
32 devices in a mesh: chan: 8 (over y, x, core), tm: 4 (over z).
Axes of the slice: x: 2, y: 2, z: 4, core: 2. Of those that a mesh axis runs over, the one named last changes fastest.
Arguments:
- signals: bfloat16 [2368, 5120], P('chan', 'tm'), may hold values from -6 to 6
- kernels: bfloat16 [2, 640], replicated, may hold values from -0.25 to 0.25
- chan_map: int32 [2368], replicated, may hold values from 0 to 2367, as said below
- crosstalk: bfloat16 [64, 37, 37], P('chan'), may hold values from -0.5 to 0.5
- starts: int32 [64, 4, 1], P(None, 'tm'), may hold values from 0 to 768
- counts: int32 [64, 4], P(None, 'tm'), may hold values from 0 to 1, as said below
Outputs:
- built: bfloat16 [64, 4, 1, 2, 37, 512], P('chan', 'tm')
Inputs may be any that keep to these rules, and one draw needn't show every extreme that they name: `chan_map`: a permutation; the rows c with (c mod (296)) // 37 = b name channels of crystals b * 8 to (b + 1) * 8 - 1 only. `counts`: some entry equals 1.
All inputs are finite; a program needn't handle non-finite values.
Results may differ from a plain program's by a relative error of at most 0.005.
Values may be sent and summed in bfloat16 or wider, within the bound.
A program may use at most 128 MiB of HBM per device.

v0:
```python
import jax
import jax.numpy as jnp
from jax import lax
from jax.sharding import PartitionSpec as P

SIG = 37
KLEN = 640
SEGLEN = 512
BLOCK = 128
SLOTS = 1
PRE = 128


def passed_along(shard, axis, by):
    length = lax.axis_size(axis)
    pairs = [(i, i + by) for i in range(length) if 0 <= i + by < length]
    return lax.ppermute(shard, axis, pairs)


def toeplitz_tables(kernels):
    span_width = KLEN + BLOCK
    row_index = lax.broadcasted_iota(jnp.int32, (span_width, BLOCK), 0)
    col_index = lax.broadcasted_iota(jnp.int32, (span_width, BLOCK), 1)
    lag_index = col_index + KLEN - row_index
    inside = jnp.logical_and(lag_index >= 0, lag_index < KLEN)
    picked = jnp.take(kernels, jnp.clip(lag_index, 0, KLEN - 1), axis=1)
    return jnp.where(inside[None], picked, jnp.zeros_like(picked))


def cut_segments(traces, row_starts):
    row_count, filter_count, samples = traces.shape
    slot_count = row_starts.shape[1]
    moving = traces[:, None]
    bit_number = 0
    while 1 << bit_number < samples:
        step_size = 1 << bit_number
        padding = jnp.zeros((row_count, slot_count, filter_count, step_size), moving.dtype)
        moved = jnp.concatenate([moving[..., step_size:], padding], axis=-1)
        take_bit = row_starts >> bit_number & 1 == 1
        moving = jnp.where(take_bit[:, :, None, None], moved, moving)
        bit_number += 1
    return moving[..., :SEGLEN]


def reorder_rows(arrived, target_rows):
    row_count = arrived.shape[0]
    flat_rows = arrived.reshape(row_count, -1)
    wanted = lax.broadcasted_iota(jnp.int32, (row_count, row_count), 0)
    permuter = (wanted == target_rows[None, :]).astype(arrived.dtype)
    placed = jnp.dot(permuter, flat_rows, preferred_element_type=jnp.float32).astype(arrived.dtype)
    return placed.reshape(arrived.shape)


def body(signals, kernels, chan_map, crosstalk, starts, counts):
    owners = lax.axis_size("chan")
    owner_index = lax.axis_index("chan")
    row_count = signals.shape[0]
    samples = signals.shape[1]
    tables = toeplitz_tables(kernels)
    tail_rows = passed_along(signals[:, samples - KLEN :], "tm", 1)
    extended = jnp.concatenate([tail_rows, signals], axis=1)
    count_blocks = samples // BLOCK
    steps_back = KLEN // BLOCK + 1
    group_rows = row_count // owners

    def filter_group(group):
        blocks = group.reshape(group_rows, count_blocks + steps_back - 1, BLOCK)
        summed = jnp.zeros((group_rows, 2, count_blocks, BLOCK), jnp.float32)
        for shift_step in range(steps_back):
            window = lax.slice_in_dim(blocks, shift_step, shift_step + count_blocks, axis=1)
            part_table = tables[:, shift_step * BLOCK : (shift_step + 1) * BLOCK, :]
            summed = summed + jnp.einsum(
                "rib,fbo->rfio", window, part_table, preferred_element_type=jnp.float32
            )
        return summed.reshape(group_rows, 2, samples).astype(jnp.bfloat16)

    grouped = extended.reshape(owners, group_rows, samples + KLEN)
    filtered = lax.map(filter_group, grouped).reshape(row_count, 2, samples)
    device_map = chan_map.reshape(owners, owners, SIG)
    sent_ids = lax.dynamic_index_in_dim(device_map, owner_index, 1, keepdims=False).reshape(
        row_count
    )
    target_rows = sent_ids - owner_index * row_count
    first_crystal = owner_index * owners
    shard_starts = starts[:, 0, :]
    own_starts = lax.dynamic_slice_in_dim(shard_starts, first_crystal, owners, 0)
    own_counts = lax.dynamic_slice_in_dim(counts[:, 0], first_crystal, owners, 0)
    arrived = lax.all_to_all(filtered, "chan", split_axis=0, concat_axis=0, tiled=True)
    ordered_traces = reorder_rows(arrived, target_rows)
    row_starts = jnp.broadcast_to(own_starts[:, None, :], (owners, SIG, SLOTS)).reshape(
        row_count, SLOTS
    )
    ordered = cut_segments(ordered_traces, row_starts)
    segments = ordered.reshape(owners, SIG, SLOTS, 2, SEGLEN)
    coupled = jnp.einsum(
        "kst,ktjfp->kjfsp", crosstalk, segments, preferred_element_type=jnp.float32
    )
    coupled = coupled + jnp.transpose(segments, (0, 2, 3, 1, 4)).astype(jnp.float32)
    center = (PRE - 1) / 2.0
    fit_axis = (jnp.arange(SEGLEN, dtype=jnp.float32) - center) / (PRE / 2.0)
    pre_axis = fit_axis[:PRE]
    offset_fit = jnp.mean(coupled[..., :PRE], axis=-1, keepdims=True)
    slope_fit = jnp.sum(coupled[..., :PRE] * pre_axis, axis=-1, keepdims=True) / jnp.sum(
        pre_axis * pre_axis
    )
    fitted = coupled - offset_fit - slope_fit * fit_axis
    live_slot = lax.broadcasted_iota(jnp.int32, (owners, SLOTS), 1) < own_counts[:, None]
    built_rows = jnp.where(
        live_slot[:, :, None, None, None], fitted, jnp.zeros_like(fitted)
    ).astype(jnp.bfloat16)
    return built_rows.reshape(owners, 1, SLOTS, 2, SIG, SEGLEN)


def solution(mesh):
    return jax.shard_map(
        body,
        mesh=mesh,
        in_specs=(
            P("chan", "tm"),
            P(),
            P(),
            P("chan", None, None),
            P(None, "tm", None),
            P(None, "tm"),
        ),
        out_specs=P("chan", "tm", None, None, None, None),
        check_vma=False,
    )
```

profile of v0, /device:TPU:1, one launch (start us, length us, event | category | flops | bytes accessed | tf_op | source)
XLA Modules:
  0.0 476.7 jit_solution(6465994442171169449)
XLA Ops:
  0.0 1.1 slice.84
  1.1 4.1 collective-permute-start
  5.3 0.9 copy.18
  6.2 343.6 %gather_fusion = bf16[98304,2]{1,0:T(8,128)(2,1)} fusion(bf16[2,640]{0,1:T(8,128)(2,1)S(1)} %copy.18, s32[98304]{0:T(1024)S(1)} %fusion.19), kind=kCustom, calls=%fused_computation | custom fusion | bytes 1179648 | tf_op jit(solution)/shard_map/jit(_take)/gather | solution.py:26
  349.7 18.8 %copy.19 = bf16[768,128,2]{1,0,2:T(8,128)(2,1)S(1)} copy(bf16[768,128,2]{2,1,0:T(8,128)(2,1)} %bitcast.126) | data formatting | bytes 786432 | tf_op jit(solution)/shard_map/jit(_take)/gather | solution.py:26
  370.1 21.6 %while.10 = (s32[]{:T(128)}, bf16[8,37,2,1280]{3,2,1,0:T(2,128)(2,1)}, bf16[8,37,1920]{2,1,0:T(8,128)(2,1)S(1)}, bf16[2,768,128]{2,1,0:T(8,128)(2,1)S(1)}, s32[]{:T(128)}) while((s32[]{:T(128)}, bf16[8,37,2,1280]{3,2,1,0:T(2,128)(2,1)}, bf16[8,37,1920]{2,1,0:T(8,128)(2,1)S(1)}, bf16[2,768,128]{2,1,0:T(8,128)(2,1)S(1)}, s32[]{:T(128)}) %tuple.39), condition=%wide.region_1.2_spmd, body=%wide.region_0.1_spmd.sunk | while | flops 146058240 | bytes 8276545 | solution.py:78
  372.0 0.8 constant_dynamic-update-slice_fusion.2
  382.8 0.8 constant_dynamic-update-slice_fusion.2
  391.8 5.0 %all-to-all-start = ((bf16[296,2,1280]{2,1,0:T(2,128)(2,1)}), bf16[296,2,1280]{2,1,0:T(2,128)(2,1)S(1)}, u32[]{:S(2)}, u32[]{:S(2)}) async-start(bf16[296,2,1280]{2,1,0:T(2,128)(2,1)} %bitcast.130), calls=%async_computation | async-start | bytes 3031040 | tf_op jit(solution)/shard_map/all_to_all | solution.py:88
  399.7 14.0 %all-to-all-done = bf16[296,2,1280]{2,1,0:T(2,128)(2,1)S(1)} async-done(((bf16[296,2,1280]{2,1,0:T(2,128)(2,1)}), bf16[296,2,1280]{2,1,0:T(2,128)(2,1)S(1)}, u32[]{:S(2)}, u32[]{:S(2)}) %all-to-all-start) | async-done | bytes 1515552 | tf_op jit(solution)/shard_map/all_to_all | solution.py:88
  413.9 1.0 convolution_convert_fusion
  415.2 3.8 slice.107
  419.0 2.7 broadcast_select_fusion
  421.7 3.8 slice.108
  425.5 2.9 broadcast_select_fusion.1
  428.4 3.8 slice.109
  432.2 2.7 broadcast_select_fusion.2
  435.0 3.8 slice.110
  438.7 3.1 broadcast_select_fusion.3
  441.9 3.8 slice.111
  445.7 2.7 broadcast_select_fusion.4
  448.4 3.8 slice.112
  452.2 2.9 broadcast_select_fusion.5
  455.1 3.8 slice.113
  458.9 2.7 broadcast_select_fusion.6
  461.6 0.9 slice.114
  462.5 2.6 broadcast_select_fusion.7
  465.2 0.8 slice.115
  466.0 2.6 broadcast_select_fusion.8
  469.2 2.5 broadcast_select_fusion.9
  471.9 1.3 broadcast_select_fusion.10
  475.2 1.3 copy.23
  (151 shorter events, 27.2 us)
Async XLA Ops:
  0.0 473.6 %copy-start = (bf16[8,37,37]{2,0,1:T(8,128)(2,1)S(1)}, bf16[8,37,37]{2,0,1:T(8,128)(2,1)}, u32[]{:S(2)}) copy-start(bf16[8,37,37]{2,0,1:T(8,128)(2,1)} %param.11) | copy-start | bytes 65716
  1.1 367.9 %collective-permute-start = (bf16[296,640]{1,0:T(8,128)(2,1)S(1)}, bf16[296,640]{1,0:T(8,128)(2,1)S(1)}, u32[]{:S(2)}, u32[]{:S(2)}) collective-permute-start(bf16[296,640]{1,0:T(8,128)(2,1)S(1)} %slice.84), channel_id=1, source_target_pairs={{0,1},{1,2},{2,3},{4,5},{5,6},{6,7},{8,9},{9,10},{10,11},{12,13},{... | collective-permute-start | bytes 1136648 | tf_op jit(solution)/shard_map/ppermute | solution.py:17
  368.6 1.1 copy-start.1
  391.8 5.0 %copy-start.3 = (s32[64,1,1]{0,2,1:T(1,128)S(1)}, s32[64,1,1]{0,2,1:T(1,128)}, u32[]{:S(2)}) copy-start(s32[64,1,1]{0,2,1:T(1,128)} %param.12) | copy-start | bytes 772
  391.8 5.3 %copy-start.2 = (s32[2368]{0:T(1024)S(1)}, s32[2368]{0:T(1024)}, u32[]{:S(2)}) copy-start(s32[2368]{0:T(1024)} %param.10) | copy-start | bytes 28420
  391.8 7.2 %copy-start.4 = (s32[64,1]{0,1:T(1,128)S(1)}, s32[64,1]{0,1:T(1,128)}, u32[]{:S(2)}) copy-start(s32[64,1]{0,1:T(1,128)} %param.13) | copy-start | bytes 772
  391.8 22.0 %all-to-all-start = ((bf16[296,2,1280]{2,1,0:T(2,128)(2,1)}), bf16[296,2,1280]{2,1,0:T(2,128)(2,1)S(1)}, u32[]{:S(2)}, u32[]{:S(2)}) async-start(bf16[296,2,1280]{2,1,0:T(2,128)(2,1)} %bitcast.130), calls=%async_computation | async-start | bytes 3031040 | tf_op jit(solution)/shard_map/all_to_all | solution.py:88
where the time goes:
time: 484 us; the launch traced here: 477 us
  local copies, waits for them, and re-layouts  410 us (85%)
  other arithmetic  31.8 us (7%)
  waiting for transfers between devices  14 us (3%)
  matrix products  10.7 us (2%)
  starting transfers between devices  9.06 us (2%)
    gather x2, local copies, waits for them, and re-layouts, toeplitz_tables(): picked = jnp.take(kernels, jnp.clip(lag_index, 0, KLEN - 1), axis=1)  362 us
    slice x11, local copies, waits for them, and re-layouts, cut_segments(): moved = jnp.concatenate([moving[..., step_size:], padding], axis=-1)  29.1 us
    select_n x11, other arithmetic, cut_segments(): moving = jnp.where(take_bit[:, :, None, None], moved, moving)  28.8 us
    all_to_all x1, waiting for transfers between devices, body(): lax.all_to_all(filtered, 'chan', split_axis=0, concat_axis=0, tiled=True)  14 us
  transfers between devices with their start and end apart: 2, of which 1 were waited for; matrix products, arithmetic and copies ran while one was open for 77% of the time, Pallas kernels for 0%

commit v1 on v0

v1 whole, which is shorter than its diff:
```python
import functools

import jax
import jax.numpy as jnp
from jax import lax
from jax.experimental import pallas as pl
from jax.experimental.pallas import tpu as pltpu
from jax.sharding import PartitionSpec as P

SEGLEN = 512
PRE = 128
LANES = 128
TILE = 16
GROUP = 256
SLOT_ROWS = 8
MESH = pl.DeviceIdType.MESH


def round_up(value, step):
    return -(-value // step) * step


def iota(shape, axis):
    return lax.broadcasted_iota(jnp.int32, shape, axis)


def kernel(
    owners, shards, x_ref, taps_ref, map_ref, cross_ref, starts_ref, counts_ref, out_ref,
    pack, arrived, placer, ordered, window, segment, table,
    chan_send, chan_recv, tail_send, tail_recv,
):
    me = lax.axis_index("chan")
    shard = lax.axis_index("tm")
    rows, samples = x_ref.shape
    klen = taps_ref.shape[1]
    crystals, sig = cross_ref.shape[0], cross_ref.shape[1]
    main = 2 * TILE
    rest = sig - main
    groups = TILE // rest
    slot = round_up(sig, SLOT_ROWS)
    height = crystals * slot
    blocks = (samples + klen) // LANES
    half_blocks = klen // LANES
    later = shard < shards - 1

    barrier = pltpu.get_barrier_semaphore()
    for step in range(1, owners):
        pl.semaphore_signal(
            barrier, inc=1, device_id={"chan": lax.rem(me + step, owners)}, device_id_type=MESH
        )

    @pl.when(shard > 0)
    def _():
        pl.semaphore_signal(barrier, inc=1, device_id={"tm": shard - 1}, device_id_type=MESH)

    def rest_row(index):
        turned = index - main
        for group in range(1, groups):
            turned = turned - jnp.where(index >= main + group * rest, rest, 0)
        return jnp.where(index < main, index, main + turned)

    for owner in range(owners):
        base = owner * sig
        low = base // TILE * TILE
        high = min(round_up(base + sig, TILE), rows)
        shape = (main + TILE, high - low)
        index = iota(shape, 0)
        wanted = base + rest_row(index)
        hit = jnp.logical_and(iota(shape, 1) + low == wanted, index < main + groups * rest)
        picker = jnp.where(hit, 1.0, 0.0).astype(jnp.bfloat16)
        picked = jnp.dot(picker, x_ref[low:high, :], preferred_element_type=jnp.float32)
        for half in range(2):
            part = picked[:, half * klen : (half + 1) * klen].astype(jnp.bfloat16)
            pack[half, owner, :, 0:klen] = part[0:TILE]
            pack[half, owner, :, klen : 2 * klen] = part[TILE:main]
            left = picked[main:, half * klen : (half + 1) * klen]
            last = left[:, 2 * GROUP : klen]
            row = iota((TILE, GROUP), 0)
            kept = jnp.where(
                row < rest,
                left[:, 0:GROUP],
                jnp.where(row < 2 * rest, left[:, GROUP : 2 * GROUP], jnp.concatenate([last, last], axis=1)),
            )
            pack[half, owner, :, 2 * klen : 2 * klen + GROUP] = kept.astype(jnp.bfloat16)

    arrived[1, me] = pack[0, me]
    arrived[2, me] = pack[1, me]

    @pl.when(shard == 0)
    def _():
        arrived[0] = jnp.zeros(arrived.shape[1:], arrived.dtype)

    pl.semaphore_wait(barrier, owners - 1 + jnp.where(later, 1, 0))

    def to_owner(half, step):
        peer = lax.rem(me + step, owners)
        return pltpu.make_async_remote_copy(
            src_ref=pack.at[half, peer],
            dst_ref=arrived.at[half + 1, me],
            send_sem=chan_send.at[half, step],
            recv_sem=chan_recv.at[half, step],
            device_id={"chan": peer},
            device_id_type=MESH,
        )

    def from_owner(half, step):
        peer = lax.rem(me + owners - step, owners)
        return pltpu.make_async_remote_copy(
            src_ref=pack.at[half, peer],
            dst_ref=arrived.at[half + 1, peer],
            send_sem=chan_send.at[half, step],
            recv_sem=chan_recv.at[half, step],
            device_id={"chan": peer},
            device_id_type=MESH,
        )

    def onward(step):
        peer = lax.rem(me + owners - step, owners)
        return pltpu.make_async_remote_copy(
            src_ref=arrived.at[2, peer],
            dst_ref=arrived.at[0, peer],
            send_sem=tail_send.at[step],
            recv_sem=tail_recv.at[step],
            device_id={"tm": jnp.minimum(shard + 1, shards - 1)},
            device_id_type=MESH,
        )

    for step in range(1, owners):
        to_owner(1, step).start()

    @pl.when(later)
    def _():
        onward(0).start()

    for step in range(1, owners):
        to_owner(0, step).start()

    taps = taps_ref[...].astype(jnp.float32)
    square = (LANES, LANES)
    upper = iota(square, 1) >= iota(square, 0)
    nothing = jnp.zeros(square, jnp.float32)
    for filter_index in range(taps.shape[0]):
        turned = []
        for block in range(half_blocks):
            row = taps[filter_index : filter_index + 1, block * LANES : (block + 1) * LANES]
            turned.append(pltpu.roll(jnp.broadcast_to(row, square), 0, 1, stride=1, stride_axis=0))
        turned.append(nothing)
        for block in range(half_blocks + 1):
            above = turned[half_blocks - block]
            below = turned[half_blocks - 1 - block] if block < half_blocks else nothing
            table[
                block * LANES : (block + 1) * LANES,
                filter_index * LANES : (filter_index + 1) * LANES,
            ] = jnp.where(upper, above, below).astype(table.dtype)

    for step in range(1, owners):
        from_owner(1, step).wait_recv()

        @pl.when(later)
        def _():
            onward(step).start()

    columns = []
    total = map_ref.shape[1]
    for source in range(owners):
        low = source * rows // LANES * LANES
        high = min(round_up((source + 1) * rows, LANES), total)
        shape = (main + TILE, high - low)
        index = iota(shape, 0)
        wanted = source * rows + me * sig + rest_row(index)
        hit = jnp.logical_and(iota(shape, 1) + low == wanted, index < main + groups * rest)
        names = map_ref[:, low:high].astype(jnp.float32) + 1.0
        columns.append(jnp.sum(jnp.where(hit, names, 0.0), axis=1, keepdims=True))
    column = jnp.concatenate(
        [c[0:TILE] for c in columns] + [c[TILE:main] for c in columns] + [c[main:] for c in columns],
        axis=0,
    )
    depth = owners * (main + TILE)
    width = round_up(height, LANES)
    lane = iota((1, width), 1)
    crystal_of = jnp.zeros((1, width), jnp.int32)
    for crystal in range(1, crystals):
        crystal_of = crystal_of + jnp.where(lane >= crystal * slot, 1, 0)
    signal_of = lane - crystal_of * slot
    wanted = jnp.where(signal_of < sig, crystal_of * sig + signal_of + me * rows + 1, -1)
    matched = jnp.where(column == wanted.astype(jnp.float32), 1.0, 0.0)
    turned = jnp.transpose(matched)[0:height]
    lane = iota((height, depth), 1)
    part_of = jnp.where(lane < owners * main, -1, lane & (TILE - 1))
    for group in range(groups):
        own = jnp.logical_and(part_of >= group * rest, part_of < (group + 1) * rest)
        keep = jnp.logical_or(part_of < 0, own)
        placer[group] = jnp.where(keep, turned, 0.0).astype(placer.dtype)

    def place(part, first_block):
        held = arrived[part].reshape(owners * TILE, arrived.shape[3])
        for group in range(groups):
            low = group * GROUP
            high = min(low + GROUP, klen)
            stacked = jnp.concatenate(
                [
                    held[:, low:high],
                    held[:, klen + low : klen + high],
                    held[:, 2 * klen : 2 * klen + high - low],
                ],
                axis=0,
            )
            rows_out = jnp.dot(placer[group], stacked, preferred_element_type=jnp.float32)
            for block in range((high - low) // LANES):
                ordered[first_block + low // LANES + block] = rows_out[
                    :, block * LANES : (block + 1) * LANES
                ]

    place(2, 2 * half_blocks)
    for step in range(1, owners):
        from_owner(0, step).wait_recv()
    place(1, half_blocks)

    @pl.when(shard > 0)
    def _():
        for step in range(owners):
            onward(step).wait_recv()

    place(0, 0)
    ordered[blocks] = jnp.zeros(ordered.shape[1:], ordered.dtype)

    window_blocks = (SEGLEN + klen) // LANES
    lane = iota((slot, LANES), 1)
    for crystal in range(crystals):
        start = starts_ref[me * crystals + crystal]
        first = start >> 7
        shift = start & (LANES - 1)
        back = (LANES - shift) & (LANES - 1)
        at = slice(crystal * slot, (crystal + 1) * slot)
        rolled = [
            pltpu.roll(ordered[first + block, at, :], back, 1) for block in range(window_blocks + 1)
        ]
        for block in range(window_blocks):
            window[block, at, :] = jnp.where(lane < LANES - shift, rolled[block], rolled[block + 1])

    steps_back = half_blocks + 1
    cut = [window[block].astype(jnp.bfloat16) for block in range(window_blocks)]
    taps_table = table[...]
    for block in range(SEGLEN // LANES):
        wide = jnp.concatenate(cut[block : block + steps_back], axis=1)
        filtered = jnp.dot(wide, taps_table, preferred_element_type=jnp.float32)
        for filter_index in range(taps.shape[0]):
            at = filter_index * SEGLEN + block * LANES
            segment[:, at : at + LANES] = filtered[
                :, filter_index * LANES : (filter_index + 1) * LANES
            ]

    center = (PRE - 1) / 2.0
    fit_axis = (iota((1, SEGLEN), 1).astype(jnp.float32) - center) / (PRE / 2.0)
    pre_axis = fit_axis[:, :PRE]
    power = jnp.sum(pre_axis * pre_axis)
    for crystal in range(crystals):
        live = counts_ref[me * crystals + crystal] > 0
        pieces = segment[crystal * slot : crystal * slot + sig, :].astype(jnp.bfloat16)
        coupled = pieces.astype(jnp.float32) + jnp.dot(
            cross_ref[crystal], pieces, preferred_element_type=jnp.float32
        )
        for filter_index in range(taps.shape[0]):
            own = coupled[:, filter_index * SEGLEN : (filter_index + 1) * SEGLEN]
            head = own[:, :PRE]
            offset_fit = jnp.mean(head, axis=1, keepdims=True)
            slope_fit = jnp.sum(head * pre_axis, axis=1, keepdims=True) / power
            fitted = own - offset_fit - slope_fit * fit_axis
            out_ref[crystal, 0, 0, filter_index] = jnp.where(live, fitted, 0.0).astype(out_ref.dtype)

    for step in range(1, owners):
        to_owner(1, step).wait_send()
        to_owner(0, step).wait_send()

    @pl.when(later)
    def _():
        for step in range(owners):
            onward(step).wait_send()


def body(signals, kernels, chan_map, crosstalk, starts, counts):
    owners = lax.axis_size("chan")
    shards = lax.axis_size("tm")
    rows, samples = signals.shape
    filters, klen = kernels.shape
    crystals, sig, _ = crosstalk.shape
    slots = starts.shape[2]
    height = crystals * round_up(sig, SLOT_ROWS)
    packed = 2 * klen + GROUP
    in_vmem = pl.BlockSpec(memory_space=pltpu.VMEM)
    in_smem = pl.BlockSpec(memory_space=pltpu.SMEM)
    return pl.pallas_call(
        functools.partial(kernel, owners, shards),
        out_shape=jax.ShapeDtypeStruct((crystals, 1, slots, filters, sig, SEGLEN), jnp.bfloat16),
        in_specs=[in_vmem] * 4 + [in_smem] * 2,
        out_specs=in_vmem,
        scratch_shapes=[
            pltpu.VMEM((2, owners, TILE, packed), jnp.bfloat16),
            pltpu.VMEM((3, owners, TILE, packed), jnp.bfloat16),
            pltpu.VMEM((TILE // (sig - 2 * TILE), height, owners * 3 * TILE), jnp.bfloat16),
            pltpu.VMEM(((samples + klen) // LANES + 1, height, LANES), jnp.float32),
            pltpu.VMEM(((SEGLEN + klen) // LANES, height, LANES), jnp.float32),
            pltpu.VMEM((height, filters * SEGLEN), jnp.float32),
            pltpu.VMEM((klen + LANES, filters * LANES), jnp.bfloat16),
            pltpu.SemaphoreType.DMA((2, owners)),
            pltpu.SemaphoreType.DMA((2, owners)),
            pltpu.SemaphoreType.DMA((owners,)),
            pltpu.SemaphoreType.DMA((owners,)),
        ],
        compiler_params=pltpu.CompilerParams(
            collective_id=0, has_side_effects=True, vmem_limit_bytes=40 * 1024 * 1024
        ),
        name="build_events",
    )(signals, kernels, chan_map.reshape(1, -1), crosstalk, starts.reshape(-1), counts.reshape(-1))


def solution(mesh):
    return jax.shard_map(
        body,
        mesh=mesh,
        in_specs=(
            P("chan", "tm"),
            P(),
            P(),
            P("chan", None, None),
            P(None, "tm", None),
            P(None, "tm"),
        ),
        out_specs=P("chan", "tm", None, None, None, None),
        check_vma=False,
    )
```

time: 484 us -> 21.7 us (0.04)
  the two profiles are of different devices: /device:TPU:1 before, /device:TPU:9 now
where the time goes in v1:
time: 21.7 us; the launch traced here: 21.4 us
  Pallas kernels  17.3 us (80%)
  local copies, waits for them, and re-layouts  4.06 us (19%)
    pallas_call x1, Pallas kernels, body(): pl.pallas_call(functools.partial(kernel, owners, shards), out_shape=jax.S...  17.3 us
    unnamed x9, local copies, waits for them, and re-layouts  2.05 us
    pallas_call x1, local copies, waits for them, and re-layouts, body(): pl.pallas_call(functools.partial(kernel, owners, shards), out_shape=jax.S...  1.29 us
    reshape x1, local copies, waits for them, and re-layouts, body(): chan_map.reshape(1, -1)  0.71 us

profile of v1, /device:TPU:9, one launch (start us, length us, event | category | flops | bytes accessed | tf_op | source)
XLA Modules:
  0.0 21.4 jit_solution(5300900152741659009)
XLA Ops:
  0.0 0.7 %reshape.9.map_ref = s32[1,2368]{1,0:T(1,128)S(1)} reshape(s32[2368]{0:T(1024)} %param.8) | data formatting | bytes 18944 | tf_op jit(solution)/shard_map/reshape | solution.py:314
  0.7 0.0 copy-start.1
  0.7 0.0 copy-start.2
  0.7 0.0 copy-start.3
  0.7 0.9 %copy.7.cross_ref = bf16[8,37,37]{2,1,0:T(8,128)(2,1)S(1)} copy(bf16[8,37,37]{2,0,1:T(8,128)(2,1)} %param.9) | data formatting | bytes 43808 | tf_op args[3]
  1.7 0.0 copy-done.1
  1.7 0.0 copy-done.2
  1.7 0.0 copy-done.3
  1.7 0.0 copy-start
  1.7 1.1 %copy-done = bf16[296,1280]{1,0:T(8,128)(2,1)S(1)} copy-done((bf16[296,1280]{1,0:T(8,128)(2,1)S(1)}, bf16[296,1280]{1,0:T(8,128)(2,1)}, u32[]{:S(2)}) %copy-start) | copy-done | bytes 757784
  2.8 17.3 %build_events.1 = bf16[8,1,1,2,37,512]{5,4,3,2,1,0:T(8,128)(2,1)S(1)} custom-call(bf16[296,1280]{1,0:T(8,128)(2,1)S(1)} %copy-done, bf16[2,640]{1,0:T(2,128)(2,1)S(1)} %copy-done.1, s32[1,2368]{1,0:T(1,128)S(1)} %reshape.9.map_ref, bf16[8,37,37]{2,1,0:T(8,128)(2,1)S(1)} %copy.7.cross_ref, s32[64]{0:T(128)S(1)} %bitcast.2, s32[64]{0:T(128)S(1)} %bitcast.3), custom_call_target="tpu_custom_call" | custom-call | tf_op jit(solution)/shard_map/build_events/pallas_call | solution.py:292
  20.1 1.3 %copy.8 = bf16[8,1,1,2,37,512]{5,3,4,2,1,0:T(2,128)(2,1)} copy(bf16[8,1,1,2,37,512]{5,4,3,2,1,0:T(8,128)(2,1)S(1)} %build_events.1) | data formatting | bytes 1212416 | tf_op jit(solution)/shard_map/build_events/pallas_call | solution.py:292
Async XLA Ops:
  0.7 1.0 %copy-start.1 = (bf16[2,640]{1,0:T(2,128)(2,1)S(1)}, bf16[2,640]{1,0:T(2,128)(2,1)}, u32[]{:S(2)}) copy-start(bf16[2,640]{1,0:T(2,128)(2,1)} %taps_ref.1) | copy-start | bytes 7684
  0.7 1.0 %copy-start.2 = (s32[64,1,1]{0,2,1:T(1,128)S(1)}, s32[64,1,1]{0,2,1:T(1,128)}, u32[]{:S(2)}) copy-start(s32[64,1,1]{0,2,1:T(1,128)} %param.10) | copy-start | bytes 772
  0.7 1.0 %copy-start.3 = (s32[64,1]{0,1:T(1,128)S(1)}, s32[64,1]{0,1:T(1,128)}, u32[]{:S(2)}) copy-start(s32[64,1]{0,1:T(1,128)} %param.11) | copy-start | bytes 772
  1.7 1.1 %copy-start = (bf16[296,1280]{1,0:T(8,128)(2,1)S(1)}, bf16[296,1280]{1,0:T(8,128)(2,1)}, u32[]{:S(2)}) copy-start(bf16[296,1280]{1,0:T(8,128)(2,1)} %x_ref.1) | copy-start | bytes 2273284

commit v2 on v1

--- a/solution.py
+++ b/solution.py
@@ -25,15 +25,15 @@
 
 
 def kernel(
-    owners, shards, x_ref, taps_ref, map_ref, cross_ref, starts_ref, counts_ref, out_ref,
-    pack, arrived, placer, ordered, window, segment, table,
-    chan_send, chan_recv, tail_send, tail_recv,
+    owners, shards, x_ref, taps_hbm, map_hbm, cross_hbm, starts_ref, counts_ref, out_ref,
+    held, taps_ref, map_ref, cross_ref, pack, arrived, placer, ordered, cross, table,
+    load_sem, small_sem, chan_send, chan_recv, tail_send, tail_recv,
 ):
     me = lax.axis_index("chan")
     shard = lax.axis_index("tm")
     rows, samples = x_ref.shape
     klen = taps_ref.shape[1]
-    crystals, sig = cross_ref.shape[0], cross_ref.shape[1]
+    sig, crystals = cross_ref.shape[0], cross_ref.shape[1]
     main = 2 * TILE
     rest = sig - main
     groups = TILE // rest
@@ -43,6 +43,22 @@
     half_blocks = klen // LANES
     later = shard < shards - 1
 
+    def load(half):
+        return pltpu.make_async_copy(
+            x_ref.at[:, half * klen : (half + 1) * klen], held.at[half], load_sem.at[half]
+        )
+
+    small = [
+        pltpu.make_async_copy(source, target, small_sem.at[at])
+        for at, (source, target) in enumerate(
+            [(taps_hbm, taps_ref), (map_hbm, map_ref), (cross_hbm, cross_ref)]
+        )
+    ]
+    load(1).start()
+    load(0).start()
+    for copy in small:
+        copy.start()
+
     barrier = pltpu.get_barrier_semaphore()
     for step in range(1, owners):
         pl.semaphore_signal(
@@ -59,21 +75,21 @@
             turned = turned - jnp.where(index >= main + group * rest, rest, 0)
         return jnp.where(index < main, index, main + turned)
 
-    for owner in range(owners):
-        base = owner * sig
-        low = base // TILE * TILE
-        high = min(round_up(base + sig, TILE), rows)
-        shape = (main + TILE, high - low)
-        index = iota(shape, 0)
-        wanted = base + rest_row(index)
-        hit = jnp.logical_and(iota(shape, 1) + low == wanted, index < main + groups * rest)
-        picker = jnp.where(hit, 1.0, 0.0).astype(jnp.bfloat16)
-        picked = jnp.dot(picker, x_ref[low:high, :], preferred_element_type=jnp.float32)
-        for half in range(2):
-            part = picked[:, half * klen : (half + 1) * klen].astype(jnp.bfloat16)
-            pack[half, owner, :, 0:klen] = part[0:TILE]
-            pack[half, owner, :, klen : 2 * klen] = part[TILE:main]
-            left = picked[main:, half * klen : (half + 1) * klen]
+    def pack_half(half):
+        load(half).wait()
+        for owner in range(owners):
+            base = owner * sig
+            low = base // TILE * TILE
+            high = min(round_up(base + sig, TILE), rows)
+            shape = (main + TILE, high - low)
+            index = iota(shape, 0)
+            wanted = base + rest_row(index)
+            hit = jnp.logical_and(iota(shape, 1) + low == wanted, index < main + groups * rest)
+            picker = jnp.where(hit, 1.0, 0.0).astype(jnp.bfloat16)
+            picked = jnp.dot(picker, held[half, low:high, :], preferred_element_type=jnp.float32)
+            pack[half, owner, :, 0:klen] = picked[0:TILE].astype(jnp.bfloat16)
+            pack[half, owner, :, klen : 2 * klen] = picked[TILE:main].astype(jnp.bfloat16)
+            left = picked[main:]
             last = left[:, 2 * GROUP : klen]
             row = iota((TILE, GROUP), 0)
             kept = jnp.where(
@@ -82,9 +98,9 @@
                 jnp.where(row < 2 * rest, left[:, GROUP : 2 * GROUP], jnp.concatenate([last, last], axis=1)),
             )
             pack[half, owner, :, 2 * klen : 2 * klen + GROUP] = kept.astype(jnp.bfloat16)
-
-    arrived[1, me] = pack[0, me]
-    arrived[2, me] = pack[1, me]
+        arrived[half + 1, me] = pack[half, me]
+
+    pack_half(1)
 
     @pl.when(shard == 0)
     def _():
@@ -132,8 +148,12 @@
     def _():
         onward(0).start()
 
+    pack_half(0)
     for step in range(1, owners):
         to_owner(0, step).start()
+
+    for copy in small:
+        copy.wait()
 
     taps = taps_ref[...].astype(jnp.float32)
     square = (LANES, LANES)
@@ -161,7 +181,7 @@
             onward(step).start()
 
     columns = []
-    total = map_ref.shape[1]
+    total = map_ref.shape[0]
     for source in range(owners):
         low = source * rows // LANES * LANES
         high = min(round_up((source + 1) * rows, LANES), total)
@@ -169,7 +189,7 @@
         index = iota(shape, 0)
         wanted = source * rows + me * sig + rest_row(index)
         hit = jnp.logical_and(iota(shape, 1) + low == wanted, index < main + groups * rest)
-        names = map_ref[:, low:high].astype(jnp.float32) + 1.0
+        names = (map_ref[low:high].astype(jnp.float32) + 1.0).reshape(1, high - low)
         columns.append(jnp.sum(jnp.where(hit, names, 0.0), axis=1, keepdims=True))
     column = jnp.concatenate(
         [c[0:TILE] for c in columns] + [c[TILE:main] for c in columns] + [c[main:] for c in columns],
@@ -185,24 +205,34 @@
     wanted = jnp.where(signal_of < sig, crystal_of * sig + signal_of + me * rows + 1, -1)
     matched = jnp.where(column == wanted.astype(jnp.float32), 1.0, 0.0)
     turned = jnp.transpose(matched)[0:height]
+    cross[...] = jnp.zeros(cross.shape, cross.dtype)
+    cross[0 : sig * crystals, 0:sig] = cross_ref[...].astype(jnp.float32).reshape(sig * crystals, sig)
+    mixed = []
+    for crystal in range(crystals):
+        own = cross[pl.ds(crystal, slot, stride=crystals), :][:, 0:slot].astype(jnp.bfloat16)
+        rows_in = turned[crystal * slot : (crystal + 1) * slot].astype(jnp.bfloat16)
+        mixed.append(jnp.dot(own, rows_in, preferred_element_type=jnp.float32))
+    mixed = jnp.concatenate(mixed, axis=0)
     lane = iota((height, depth), 1)
     part_of = jnp.where(lane < owners * main, -1, lane & (TILE - 1))
     for group in range(groups):
         own = jnp.logical_and(part_of >= group * rest, part_of < (group + 1) * rest)
         keep = jnp.logical_or(part_of < 0, own)
-        placer[group] = jnp.where(keep, turned, 0.0).astype(placer.dtype)
+        placer[group, :, 0:depth] = jnp.where(keep, turned, 0.0).astype(placer.dtype)
+        placer[group, :, depth : 2 * depth] = jnp.where(keep, mixed, 0.0).astype(placer.dtype)
 
     def place(part, first_block):
-        held = arrived[part].reshape(owners * TILE, arrived.shape[3])
+        source = arrived[part].reshape(owners * TILE, arrived.shape[3])
         for group in range(groups):
             low = group * GROUP
             high = min(low + GROUP, klen)
             stacked = jnp.concatenate(
                 [
-                    held[:, low:high],
-                    held[:, klen + low : klen + high],
-                    held[:, 2 * klen : 2 * klen + high - low],
-                ],
+                    source[:, low:high],
+                    source[:, klen + low : klen + high],
+                    source[:, 2 * klen : 2 * klen + high - low],
+                ]
+                * 2,
                 axis=0,
             )
             rows_out = jnp.dot(placer[group], stacked, preferred_element_type=jnp.float32)
@@ -225,48 +255,60 @@
     ordered[blocks] = jnp.zeros(ordered.shape[1:], ordered.dtype)
 
     window_blocks = (SEGLEN + klen) // LANES
+    seg_blocks = SEGLEN // LANES
+    steps_back = half_blocks + 1
     lane = iota((slot, LANES), 1)
-    for crystal in range(crystals):
-        start = starts_ref[me * crystals + crystal]
-        first = start >> 7
-        shift = start & (LANES - 1)
-        back = (LANES - shift) & (LANES - 1)
-        at = slice(crystal * slot, (crystal + 1) * slot)
-        rolled = [
-            pltpu.roll(ordered[first + block, at, :], back, 1) for block in range(window_blocks + 1)
+    center = (PRE - 1) / 2.0
+    fit_axis = [
+        (iota((1, LANES), 1).astype(jnp.float32) + (block * LANES - center)) / (PRE / 2.0)
+        for block in range(seg_blocks)
+    ]
+    pre_axis = fit_axis[0]
+    power = jnp.sum(pre_axis * pre_axis)
+    taps_table = table[...]
+    pair = 2 if crystals % 2 == 0 else 1
+    high = pair * slot
+    for crystal in range(0, crystals, pair):
+        windows = []
+        for member in range(crystal, crystal + pair):
+            start = starts_ref[me * crystals + member]
+            first = start >> 7
+            shift = start & (LANES - 1)
+            back = (LANES - shift) & (LANES - 1)
+            at = slice(member * slot, (member + 1) * slot)
+            rolled = [
+                pltpu.roll(ordered[first + block, at, :], back, 1)
+                for block in range(window_blocks + 1)
+            ]
+            windows.append(
+                [
+                    jnp.where(lane < LANES - shift, rolled[block], rolled[block + 1])
+                    for block in range(window_blocks)
+                ]
+            )
+        cut = [
+            jnp.concatenate([w[block] for w in windows], axis=0).astype(jnp.bfloat16)
+            for block in range(window_blocks)
         ]
-        for block in range(window_blocks):
-            window[block, at, :] = jnp.where(lane < LANES - shift, rolled[block], rolled[block + 1])
-
-    steps_back = half_blocks + 1
-    cut = [window[block].astype(jnp.bfloat16) for block in range(window_blocks)]
-    taps_table = table[...]
-    for block in range(SEGLEN // LANES):
-        wide = jnp.concatenate(cut[block : block + steps_back], axis=1)
-        filtered = jnp.dot(wide, taps_table, preferred_element_type=jnp.float32)
+        wide = jnp.concatenate(
+            [jnp.concatenate(cut[b : b + steps_back], axis=1) for b in range(seg_blocks)], axis=0
+        )
+        coupled = jnp.dot(wide, taps_table, preferred_element_type=jnp.float32)
         for filter_index in range(taps.shape[0]):
-            at = filter_index * SEGLEN + block * LANES
-            segment[:, at : at + LANES] = filtered[
-                :, filter_index * LANES : (filter_index + 1) * LANES
+            own = [
+                coupled[b * high : (b + 1) * high, filter_index * LANES : (filter_index + 1) * LANES]
+                for b in range(seg_blocks)
             ]
-
-    center = (PRE - 1) / 2.0
-    fit_axis = (iota((1, SEGLEN), 1).astype(jnp.float32) - center) / (PRE / 2.0)
-    pre_axis = fit_axis[:, :PRE]
-    power = jnp.sum(pre_axis * pre_axis)
-    for crystal in range(crystals):
-        live = counts_ref[me * crystals + crystal] > 0
-        pieces = segment[crystal * slot : crystal * slot + sig, :].astype(jnp.bfloat16)
-        coupled = pieces.astype(jnp.float32) + jnp.dot(
-            cross_ref[crystal], pieces, preferred_element_type=jnp.float32
-        )
-        for filter_index in range(taps.shape[0]):
-            own = coupled[:, filter_index * SEGLEN : (filter_index + 1) * SEGLEN]
-            head = own[:, :PRE]
-            offset_fit = jnp.mean(head, axis=1, keepdims=True)
-            slope_fit = jnp.sum(head * pre_axis, axis=1, keepdims=True) / power
-            fitted = own - offset_fit - slope_fit * fit_axis
-            out_ref[crystal, 0, 0, filter_index] = jnp.where(live, fitted, 0.0).astype(out_ref.dtype)
+            offset_fit = jnp.mean(own[0], axis=1, keepdims=True)
+            slope_fit = jnp.sum(own[0] * pre_axis, axis=1, keepdims=True) / power
+            for b in range(seg_blocks):
+                fitted = own[b] - offset_fit - slope_fit * fit_axis[b]
+                for member in range(pair):
+                    live = counts_ref[me * crystals + crystal + member] > 0
+                    kept = fitted[member * slot : member * slot + sig]
+                    out_ref[
+                        crystal + member, 0, 0, filter_index, :, b * LANES : (b + 1) * LANES
+                    ] = jnp.where(live, kept, 0.0).astype(out_ref.dtype)
 
     for step in range(1, owners):
         to_owner(1, step).wait_send()
@@ -289,29 +331,35 @@
     packed = 2 * klen + GROUP
     in_vmem = pl.BlockSpec(memory_space=pltpu.VMEM)
     in_smem = pl.BlockSpec(memory_space=pltpu.SMEM)
+    in_hbm = pl.BlockSpec(memory_space=pltpu.HBM)
     return pl.pallas_call(
         functools.partial(kernel, owners, shards),
         out_shape=jax.ShapeDtypeStruct((crystals, 1, slots, filters, sig, SEGLEN), jnp.bfloat16),
-        in_specs=[in_vmem] * 4 + [in_smem] * 2,
+        in_specs=[in_hbm] * 4 + [in_smem] * 2,
         out_specs=in_vmem,
         scratch_shapes=[
+            pltpu.VMEM((2, rows, klen), jnp.bfloat16),
+            pltpu.VMEM(kernels.shape, kernels.dtype),
+            pltpu.VMEM(chan_map.shape, chan_map.dtype),
+            pltpu.VMEM((sig, crystals, sig), crosstalk.dtype),
             pltpu.VMEM((2, owners, TILE, packed), jnp.bfloat16),
             pltpu.VMEM((3, owners, TILE, packed), jnp.bfloat16),
-            pltpu.VMEM((TILE // (sig - 2 * TILE), height, owners * 3 * TILE), jnp.bfloat16),
+            pltpu.VMEM((TILE // (sig - 2 * TILE), height, 2 * owners * 3 * TILE), jnp.bfloat16),
             pltpu.VMEM(((samples + klen) // LANES + 1, height, LANES), jnp.float32),
-            pltpu.VMEM(((SEGLEN + klen) // LANES, height, LANES), jnp.float32),
-            pltpu.VMEM((height, filters * SEGLEN), jnp.float32),
+            pltpu.VMEM((height, LANES), jnp.float32),
             pltpu.VMEM((klen + LANES, filters * LANES), jnp.bfloat16),
+            pltpu.SemaphoreType.DMA((2,)),
+            pltpu.SemaphoreType.DMA((3,)),
             pltpu.SemaphoreType.DMA((2, owners)),
             pltpu.SemaphoreType.DMA((2, owners)),
             pltpu.SemaphoreType.DMA((owners,)),
             pltpu.SemaphoreType.DMA((owners,)),
         ],
         compiler_params=pltpu.CompilerParams(
-            collective_id=0, has_side_effects=True, vmem_limit_bytes=40 * 1024 * 1024
+            collective_id=0, has_side_effects=True, vmem_limit_bytes=62 * 1024 * 1024
         ),
         name="build_events",
-    )(signals, kernels, chan_map.reshape(1, -1), crosstalk, starts.reshape(-1), counts.reshape(-1))
+    )(signals, kernels, chan_map, jnp.transpose(crosstalk, (1, 0, 2)), starts.reshape(-1), counts.reshape(-1))
 
 
 def solution(mesh):

time: 21.7 us -> 20.9 us (0.963)
  the two profiles are of different devices: /device:TPU:9 before, /device:TPU:17 now
where the time goes in v2:
time: 20.9 us; the launch traced here: 20.7 us
  Pallas kernels  18.3 us (88%)
  local copies, waits for them, and re-layouts  2.38 us (11%)
    pallas_call x1, Pallas kernels, body(): pl.pallas_call(functools.partial(kernel, owners, shards), out_shape=jax.S...  18.3 us
    pallas_call x1, local copies, waits for them, and re-layouts, body(): pl.pallas_call(functools.partial(kernel, owners, shards), out_shape=jax.S...  2.38 us

profile of v2, /device:TPU:17, one launch (start us, length us, event | category | flops | bytes accessed | tf_op | source)
XLA Modules:
  0.0 20.7 jit_solution(6510700190058271244)
XLA Ops:
  0.0 18.3 %build_events.1 = bf16[8,1,1,2,37,512]{5,4,3,2,1,0:T(8,128)(2,1)} custom-call(bf16[296,1280]{1,0:T(8,128)(2,1)} %x_ref.1, bf16[2,640]{1,0:T(2,128)(2,1)} %taps_hbm.1, s32[2368]{0:T(1024)} %map_hbm.1, bf16[37,8,37]{2,1,0:T(8,128)(2,1)} %bitcast.3, s32[64]{0:T(128)} %bitcast.4, s32[64]{0:T(128)} %bitcast.5), custom_call_target="tpu_custom_call" | custom-call | tf_op jit(solution)/shard_map/build_events/pallas_call | solution.py:335
  18.3 2.4 %copy.7 = bf16[8,1,1,2,37,512]{5,3,4,2,1,0:T(2,128)(2,1)} copy(bf16[8,1,1,2,37,512]{5,4,3,2,1,0:T(8,128)(2,1)} %build_events.1) | data formatting | bytes 1212416 | tf_op jit(solution)/shard_map/build_events/pallas_call | solution.py:335

commit v3 on v2

--- a/solution.py
+++ b/solution.py
@@ -24,10 +24,9 @@
     return lax.broadcasted_iota(jnp.int32, shape, axis)
 
 
-def kernel(
-    owners, shards, x_ref, taps_hbm, map_hbm, cross_hbm, starts_ref, counts_ref, out_ref,
-    held, taps_ref, map_ref, cross_ref, pack, arrived, placer, ordered, cross, table,
-    load_sem, small_sem, chan_send, chan_recv, tail_send, tail_recv,
+def gather_kernel(
+    owners, shards, x_ref, taps_ref, map_ref, cross_ref, ordered, table, coupling,
+    pack, arrived, placer, cross, chan_send, chan_recv, tail_send, tail_recv,
 ):
     me = lax.axis_index("chan")
     shard = lax.axis_index("tm")
@@ -43,26 +42,18 @@
     half_blocks = klen // LANES
     later = shard < shards - 1
 
-    def load(half):
-        return pltpu.make_async_copy(
-            x_ref.at[:, half * klen : (half + 1) * klen], held.at[half], load_sem.at[half]
-        )
-
-    small = [
-        pltpu.make_async_copy(source, target, small_sem.at[at])
-        for at, (source, target) in enumerate(
-            [(taps_hbm, taps_ref), (map_hbm, map_ref), (cross_hbm, cross_ref)]
-        )
-    ]
-    load(1).start()
-    load(0).start()
-    for copy in small:
-        copy.start()
+    def partner(step):
+        if owners & (owners - 1) == 0:
+            return me ^ step, me ^ step
+        return lax.rem(me + step, owners), lax.rem(me + owners - step, owners)
+
+    steps = [step for low in range(2) for step in range(low, owners, 2)]
+    steps = [1] + [step for step in steps if step > 1] if owners > 1 else []
 
     barrier = pltpu.get_barrier_semaphore()
     for step in range(1, owners):
         pl.semaphore_signal(
-            barrier, inc=1, device_id={"chan": lax.rem(me + step, owners)}, device_id_type=MESH
+            barrier, inc=1, device_id={"chan": partner(step)[0]}, device_id_type=MESH
         )
 
     @pl.when(shard > 0)
@@ -76,7 +67,6 @@
         return jnp.where(index < main, index, main + turned)
 
     def pack_half(half):
-        load(half).wait()
         for owner in range(owners):
             base = owner * sig
             low = base // TILE * TILE
@@ -86,7 +76,7 @@
             wanted = base + rest_row(index)
             hit = jnp.logical_and(iota(shape, 1) + low == wanted, index < main + groups * rest)
             picker = jnp.where(hit, 1.0, 0.0).astype(jnp.bfloat16)
-            picked = jnp.dot(picker, held[half, low:high, :], preferred_element_type=jnp.float32)
+            picked = jnp.dot(picker, x_ref[low:high, half * klen : (half + 1) * klen], preferred_element_type=jnp.float32)
             pack[half, owner, :, 0:klen] = picked[0:TILE].astype(jnp.bfloat16)
             pack[half, owner, :, klen : 2 * klen] = picked[TILE:main].astype(jnp.bfloat16)
             left = picked[main:]
@@ -109,7 +99,7 @@
     pl.semaphore_wait(barrier, owners - 1 + jnp.where(later, 1, 0))
 
     def to_owner(half, step):
-        peer = lax.rem(me + step, owners)
+        peer = partner(step)[0]
         return pltpu.make_async_remote_copy(
             src_ref=pack.at[half, peer],
             dst_ref=arrived.at[half + 1, me],
@@ -120,7 +110,7 @@
         )
 
     def from_owner(half, step):
-        peer = lax.rem(me + owners - step, owners)
+        peer = partner(step)[1]
         return pltpu.make_async_remote_copy(
             src_ref=pack.at[half, peer],
             dst_ref=arrived.at[half + 1, peer],
@@ -131,7 +121,7 @@
         )
 
     def onward(step):
-        peer = lax.rem(me + owners - step, owners)
+        peer = partner(step)[1] if step else me
         return pltpu.make_async_remote_copy(
             src_ref=arrived.at[2, peer],
             dst_ref=arrived.at[0, peer],
@@ -141,7 +131,7 @@
             device_id_type=MESH,
         )
 
-    for step in range(1, owners):
+    for step in steps:
         to_owner(1, step).start()
 
     @pl.when(later)
@@ -149,11 +139,8 @@
         onward(0).start()
 
     pack_half(0)
-    for step in range(1, owners):
+    for step in steps:
         to_owner(0, step).start()
-
-    for copy in small:
-        copy.wait()
 
     taps = taps_ref[...].astype(jnp.float32)
     square = (LANES, LANES)
@@ -173,7 +160,7 @@
                 filter_index * LANES : (filter_index + 1) * LANES,
             ] = jnp.where(upper, above, below).astype(table.dtype)
 
-    for step in range(1, owners):
+    for step in steps:
         from_owner(1, step).wait_recv()
 
         @pl.when(later)
@@ -207,19 +194,14 @@
     turned = jnp.transpose(matched)[0:height]
     cross[...] = jnp.zeros(cross.shape, cross.dtype)
     cross[0 : sig * crystals, 0:sig] = cross_ref[...].astype(jnp.float32).reshape(sig * crystals, sig)
-    mixed = []
     for crystal in range(crystals):
-        own = cross[pl.ds(crystal, slot, stride=crystals), :][:, 0:slot].astype(jnp.bfloat16)
-        rows_in = turned[crystal * slot : (crystal + 1) * slot].astype(jnp.bfloat16)
-        mixed.append(jnp.dot(own, rows_in, preferred_element_type=jnp.float32))
-    mixed = jnp.concatenate(mixed, axis=0)
+        coupling[crystal] = cross[pl.ds(crystal, slot, stride=crystals), :]
     lane = iota((height, depth), 1)
     part_of = jnp.where(lane < owners * main, -1, lane & (TILE - 1))
     for group in range(groups):
         own = jnp.logical_and(part_of >= group * rest, part_of < (group + 1) * rest)
         keep = jnp.logical_or(part_of < 0, own)
-        placer[group, :, 0:depth] = jnp.where(keep, turned, 0.0).astype(placer.dtype)
-        placer[group, :, depth : 2 * depth] = jnp.where(keep, mixed, 0.0).astype(placer.dtype)
+        placer[group] = jnp.where(keep, turned, 0.0).astype(placer.dtype)
 
     def place(part, first_block):
         source = arrived[part].reshape(owners * TILE, arrived.shape[3])
@@ -231,8 +213,7 @@
                     source[:, low:high],
                     source[:, klen + low : klen + high],
                     source[:, 2 * klen : 2 * klen + high - low],
-                ]
-                * 2,
+                ],
                 axis=0,
             )
             rows_out = jnp.dot(placer[group], stacked, preferred_element_type=jnp.float32)
@@ -242,7 +223,7 @@
                 ]
 
     place(2, 2 * half_blocks)
-    for step in range(1, owners):
+    for step in steps:
         from_owner(0, step).wait_recv()
     place(1, half_blocks)
 
@@ -253,6 +234,25 @@
 
     place(0, 0)
     ordered[blocks] = jnp.zeros(ordered.shape[1:], ordered.dtype)
+
+    for step in steps:
+        to_owner(1, step).wait_send()
+        to_owner(0, step).wait_send()
+
+    @pl.when(later)
+    def _():
+        for step in range(owners):
+            onward(step).wait_send()
+
+
+def build_kernel(
+    sig, ordered, table, coupling, starts_ref, counts_ref, out_ref, rows_of, built, out_sem
+):
+    me = lax.axis_index("chan")
+    crystals, slot = coupling.shape[0], coupling.shape[1]
+    filters = table.shape[1] // LANES
+    half_blocks = table.shape[0] // LANES - 1
+    klen = half_blocks * LANES
 
     window_blocks = (SEGLEN + klen) // LANES
     seg_blocks = SEGLEN // LANES
@@ -293,31 +293,37 @@
         wide = jnp.concatenate(
             [jnp.concatenate(cut[b : b + steps_back], axis=1) for b in range(seg_blocks)], axis=0
         )
-        coupled = jnp.dot(wide, taps_table, preferred_element_type=jnp.float32)
-        for filter_index in range(taps.shape[0]):
-            own = [
-                coupled[b * high : (b + 1) * high, filter_index * LANES : (filter_index + 1) * LANES]
-                for b in range(seg_blocks)
-            ]
-            offset_fit = jnp.mean(own[0], axis=1, keepdims=True)
-            slope_fit = jnp.sum(own[0] * pre_axis, axis=1, keepdims=True) / power
-            for b in range(seg_blocks):
-                fitted = own[b] - offset_fit - slope_fit * fit_axis[b]
-                for member in range(pair):
-                    live = counts_ref[me * crystals + crystal + member] > 0
-                    kept = fitted[member * slot : member * slot + sig]
-                    out_ref[
-                        crystal + member, 0, 0, filter_index, :, b * LANES : (b + 1) * LANES
-                    ] = jnp.where(live, kept, 0.0).astype(out_ref.dtype)
-
-    for step in range(1, owners):
-        to_owner(1, step).wait_send()
-        to_owner(0, step).wait_send()
-
-    @pl.when(later)
-    def _():
-        for step in range(owners):
-            onward(step).wait_send()
+        filtered = jnp.dot(wide, taps_table, preferred_element_type=jnp.float32)
+        for member in range(pair):
+            at = crystal + member
+            live = counts_ref[me * crystals + at] > 0
+            pieces = jnp.concatenate(
+                [
+                    filtered[b * high + member * slot : b * high + (member + 1) * slot]
+                    for b in range(seg_blocks)
+                ],
+                axis=1,
+            ).astype(jnp.bfloat16)
+            mixer = coupling[at][:, 0:slot].astype(jnp.bfloat16)
+            coupled = pieces.astype(jnp.float32) + jnp.dot(
+                mixer, pieces, preferred_element_type=jnp.float32
+            )
+            for filter_index in range(filters):
+                own = [
+                    coupled[:, (b * filters + filter_index) * LANES :][:, :LANES]
+                    for b in range(seg_blocks)
+                ]
+                offset_fit = jnp.mean(own[0], axis=1, keepdims=True)
+                slope_fit = jnp.sum(own[0] * pre_axis, axis=1, keepdims=True) / power
+                for b in range(seg_blocks):
+                    fitted = own[b] - offset_fit - slope_fit * fit_axis[b]
+                    rows_of[
+                        at, pl.ds(b * filters + filter_index, slot, stride=filters * seg_blocks), :
+                    ] = jnp.where(live, fitted, 0.0)
+            built[at] = rows_of[at, 0 : built.shape[1], :].astype(built.dtype)
+            pltpu.make_async_copy(built.at[at], out_ref.at[at], out_sem.at[at]).start()
+    for at in range(crystals):
+        pltpu.make_async_copy(built.at[at], out_ref.at[at], out_sem.at[at]).wait()
 
 
 def body(signals, kernels, chan_map, crosstalk, starts, counts):
@@ -327,39 +333,52 @@
     filters, klen = kernels.shape
     crystals, sig, _ = crosstalk.shape
     slots = starts.shape[2]
-    height = crystals * round_up(sig, SLOT_ROWS)
+    slot = round_up(sig, SLOT_ROWS)
+    height = crystals * slot
     packed = 2 * klen + GROUP
+    blocks = SEGLEN // LANES
     in_vmem = pl.BlockSpec(memory_space=pltpu.VMEM)
     in_smem = pl.BlockSpec(memory_space=pltpu.SMEM)
     in_hbm = pl.BlockSpec(memory_space=pltpu.HBM)
-    return pl.pallas_call(
-        functools.partial(kernel, owners, shards),
-        out_shape=jax.ShapeDtypeStruct((crystals, 1, slots, filters, sig, SEGLEN), jnp.bfloat16),
-        in_specs=[in_hbm] * 4 + [in_smem] * 2,
-        out_specs=in_vmem,
+    ordered, table, coupling = pl.pallas_call(
+        functools.partial(gather_kernel, owners, shards),
+        out_shape=(
+            jax.ShapeDtypeStruct(((samples + klen) // LANES + 1, height, LANES), jnp.float32),
+            jax.ShapeDtypeStruct((klen + LANES, filters * LANES), jnp.bfloat16),
+            jax.ShapeDtypeStruct((crystals, slot, LANES), jnp.float32),
+        ),
+        in_specs=[in_vmem] * 4,
+        out_specs=(in_vmem,) * 3,
         scratch_shapes=[
-            pltpu.VMEM((2, rows, klen), jnp.bfloat16),
-            pltpu.VMEM(kernels.shape, kernels.dtype),
-            pltpu.VMEM(chan_map.shape, chan_map.dtype),
-            pltpu.VMEM((sig, crystals, sig), crosstalk.dtype),
             pltpu.VMEM((2, owners, TILE, packed), jnp.bfloat16),
             pltpu.VMEM((3, owners, TILE, packed), jnp.bfloat16),
-            pltpu.VMEM((TILE // (sig - 2 * TILE), height, 2 * owners * 3 * TILE), jnp.bfloat16),
-            pltpu.VMEM(((samples + klen) // LANES + 1, height, LANES), jnp.float32),
+            pltpu.VMEM((TILE // (sig - 2 * TILE), height, owners * 3 * TILE), jnp.bfloat16),
             pltpu.VMEM((height, LANES), jnp.float32),
-            pltpu.VMEM((klen + LANES, filters * LANES), jnp.bfloat16),
-            pltpu.SemaphoreType.DMA((2,)),
-            pltpu.SemaphoreType.DMA((3,)),
             pltpu.SemaphoreType.DMA((2, owners)),
             pltpu.SemaphoreType.DMA((2, owners)),
             pltpu.SemaphoreType.DMA((owners,)),
             pltpu.SemaphoreType.DMA((owners,)),
         ],
         compiler_params=pltpu.CompilerParams(
-            collective_id=0, has_side_effects=True, vmem_limit_bytes=62 * 1024 * 1024
+            collective_id=0, has_side_effects=True, vmem_limit_bytes=32 * 1024 * 1024
         ),
+        name="gather_rows",
+    )(signals, kernels, chan_map, jnp.transpose(crosstalk, (1, 0, 2)))
+    built = pl.pallas_call(
+        functools.partial(build_kernel, sig),
+        out_shape=jax.ShapeDtypeStruct((crystals, sig * blocks * filters, LANES), jnp.bfloat16),
+        in_specs=[in_vmem] * 3 + [in_smem] * 2,
+        out_specs=in_hbm,
+        scratch_shapes=[
+            pltpu.VMEM((crystals, slot * blocks * filters, LANES), jnp.float32),
+            pltpu.VMEM((crystals, sig * blocks * filters, LANES), jnp.bfloat16),
+            pltpu.SemaphoreType.DMA((crystals,)),
+        ],
+        compiler_params=pltpu.CompilerParams(vmem_limit_bytes=32 * 1024 * 1024),
         name="build_events",
-    )(signals, kernels, chan_map, jnp.transpose(crosstalk, (1, 0, 2)), starts.reshape(-1), counts.reshape(-1))
+    )(ordered, table, coupling, starts.reshape(-1), counts.reshape(-1))
+    parts = built.reshape(crystals, sig, blocks, filters, LANES)
+    return jnp.transpose(parts, (0, 3, 1, 2, 4)).reshape(crystals, 1, slots, filters, sig, SEGLEN)
 
 
 def solution(mesh):

time: 20.9 us -> 23.2 us (1.11)
  the two profiles are of different devices: /device:TPU:17 before, /device:TPU:1 now
where the time goes in v3:
time: 23.2 us; the launch traced here: 22.9 us
  Pallas kernels  18.1 us (78%)
  local copies, waits for them, and re-layouts  4.7 us (20%)
    pallas_call x1, Pallas kernels, body(): pl.pallas_call(functools.partial(gather_kernel, owners, shards), out_shap...  15 us
    unnamed x12, local copies, waits for them, and re-layouts  4.7 us
    pallas_call x1, Pallas kernels, body(): pl.pallas_call(functools.partial(build_kernel, sig), out_shape=jax.ShapeD...  3.17 us

profile of v3, /device:TPU:1, one launch (start us, length us, event | category | flops | bytes accessed | tf_op | source)
XLA Modules:
  0.0 22.9 jit_solution(10233959705210224691)
XLA Ops:
  0.0 0.0 copy-start
  0.0 1.1 %copy-done = bf16[296,1280]{1,0:T(8,128)(2,1)S(1)} copy-done((bf16[296,1280]{1,0:T(8,128)(2,1)S(1)}, bf16[296,1280]{1,0:T(8,128)(2,1)}, u32[]{:S(2)}) %copy-start) | copy-done | bytes 757784
  1.1 0.0 copy-start.1
  1.1 0.9 %copy-done.1 = bf16[8,37,37]{2,0,1:T(8,128)(2,1)S(1)} copy-done((bf16[8,37,37]{2,0,1:T(8,128)(2,1)S(1)}, bf16[8,37,37]{2,0,1:T(8,128)(2,1)}, u32[]{:S(2)}) %copy-start.1) | copy-done | bytes 21928
  2.0 0.0 copy-start.2
  2.0 0.7 %copy-done.2 = s32[2368]{0:T(1024)S(1)} copy-done((s32[2368]{0:T(1024)S(1)}, s32[2368]{0:T(1024)}, u32[]{:S(2)}) %copy-start.2) | copy-done | bytes 9496
  2.7 0.0 copy-start.3
  2.7 0.7 %copy-done.3 = bf16[2,640]{1,0:T(2,128)(2,1)S(1)} copy-done((bf16[2,640]{1,0:T(2,128)(2,1)S(1)}, bf16[2,640]{1,0:T(2,128)(2,1)}, u32[]{:S(2)}) %copy-start.3) | copy-done | bytes 2584
  3.4 15.0 %gather_rows.1 = (f32[16,320,128]{2,1,0:T(8,128)S(1)}, bf16[768,256]{1,0:T(8,128)(2,1)S(1)}, f32[8,40,128]{2,1,0:T(8,128)S(1)}) custom-call(bf16[296,1280]{1,0:T(8,128)(2,1)S(1)} %copy-done, bf16[2,640]{1,0:T(2,128)(2,1)S(1)} %copy-done.3, s32[2368]{0:T(1024)S(1)} %copy-done.2, bf16[37,8,37]{2,1,0:T(8,128)(2,1)S(1)} %bitcast.8), custom_call_target="tpu_custom_call" | custom-call | tf_op jit(solution)/shard_map/gather_rows/pallas_call | solution.py:343
  18.4 0.0 copy-start.4
  18.4 0.6 %copy-done.4 = s32[64,1,1]{0,2,1:T(1,128)S(1)} copy-done((s32[64,1,1]{0,2,1:T(1,128)S(1)}, s32[64,1,1]{0,2,1:T(1,128)}, u32[]{:S(2)}) %copy-start.4) | copy-done | bytes 280
  19.0 0.0 copy-start.5
  19.0 0.7 %copy-done.5 = s32[64,1]{0,1:T(1,128)S(1)} copy-done((s32[64,1]{0,1:T(1,128)S(1)}, s32[64,1]{0,1:T(1,128)}, u32[]{:S(2)}) %copy-start.5) | copy-done | bytes 280
  19.7 3.2 %build_events.1 = bf16[8,296,128]{2,1,0:T(8,128)(2,1)} custom-call(f32[16,320,128]{2,1,0:T(8,128)S(1)} %get-tuple-element.8.ordered, bf16[768,256]{1,0:T(8,128)(2,1)S(1)} %get-tuple-element.9.table, f32[8,40,128]{2,1,0:T(8,128)S(1)} %get-tuple-element.10.coupling, s32[64]{0:T(128)S(1)} %bitcast.9, s32[64]{0:T(128)S(1)} %bitcast.10), custom_call_target="tpu_custom_call" | custom-call | tf_op jit(solution)/shard_map/build_events/pallas_call | solution.py:367
Async XLA Ops:
  0.0 1.1 %copy-start = (bf16[296,1280]{1,0:T(8,128)(2,1)S(1)}, bf16[296,1280]{1,0:T(8,128)(2,1)}, u32[]{:S(2)}) copy-start(bf16[296,1280]{1,0:T(8,128)(2,1)} %x_ref.1) | copy-start | bytes 2273284
  1.1 0.9 %copy-start.1 = (bf16[8,37,37]{2,0,1:T(8,128)(2,1)S(1)}, bf16[8,37,37]{2,0,1:T(8,128)(2,1)}, u32[]{:S(2)}) copy-start(bf16[8,37,37]{2,0,1:T(8,128)(2,1)} %param.9) | copy-start | bytes 65716
  2.0 0.7 %copy-start.2 = (s32[2368]{0:T(1024)S(1)}, s32[2368]{0:T(1024)}, u32[]{:S(2)}) copy-start(s32[2368]{0:T(1024)} %map_ref.1) | copy-start | bytes 28420
  2.7 0.7 %copy-start.3 = (bf16[2,640]{1,0:T(2,128)(2,1)S(1)}, bf16[2,640]{1,0:T(2,128)(2,1)}, u32[]{:S(2)}) copy-start(bf16[2,640]{1,0:T(2,128)(2,1)} %taps_ref.1) | copy-start | bytes 7684
  18.4 0.7 %copy-start.4 = (s32[64,1,1]{0,2,1:T(1,128)S(1)}, s32[64,1,1]{0,2,1:T(1,128)}, u32[]{:S(2)}) copy-start(s32[64,1,1]{0,2,1:T(1,128)} %param.10) | copy-start | bytes 772
  19.0 0.7 %copy-start.5 = (s32[64,1]{0,1:T(1,128)S(1)}, s32[64,1]{0,1:T(1,128)}, u32[]{:S(2)}) copy-start(s32[64,1]{0,1:T(1,128)} %param.11) | copy-start | bytes 772

commit v4 on v3

--- a/solution.py
+++ b/solution.py
@@ -24,9 +24,10 @@
     return lax.broadcasted_iota(jnp.int32, shape, axis)
 
 
-def gather_kernel(
-    owners, shards, x_ref, taps_ref, map_ref, cross_ref, ordered, table, coupling,
-    pack, arrived, placer, cross, chan_send, chan_recv, tail_send, tail_recv,
+def kernel(
+    owners, shards, x_ref, taps_hbm, map_hbm, cross_hbm, starts_ref, counts_ref, out_ref,
+    held, taps_ref, map_ref, cross_ref, pack, arrived, placer, ordered, cross, table, rows_of, built,
+    load_sem, small_sem, chan_send, chan_recv, tail_send, tail_recv, out_sem,
 ):
     me = lax.axis_index("chan")
     shard = lax.axis_index("tm")
@@ -42,6 +43,22 @@
     half_blocks = klen // LANES
     later = shard < shards - 1
 
+    def load(half):
+        return pltpu.make_async_copy(
+            x_ref.at[:, half * klen : (half + 1) * klen], held.at[half], load_sem.at[half]
+        )
+
+    small = [
+        pltpu.make_async_copy(source, target, small_sem.at[at])
+        for at, (source, target) in enumerate(
+            [(taps_hbm, taps_ref), (map_hbm, map_ref), (cross_hbm, cross_ref)]
+        )
+    ]
+    load(1).start()
+    load(0).start()
+    for copy in small:
+        copy.start()
+
     def partner(step):
         if owners & (owners - 1) == 0:
             return me ^ step, me ^ step
@@ -67,6 +84,7 @@
         return jnp.where(index < main, index, main + turned)
 
     def pack_half(half):
+        load(half).wait()
         for owner in range(owners):
             base = owner * sig
             low = base // TILE * TILE
@@ -76,7 +94,7 @@
             wanted = base + rest_row(index)
             hit = jnp.logical_and(iota(shape, 1) + low == wanted, index < main + groups * rest)
             picker = jnp.where(hit, 1.0, 0.0).astype(jnp.bfloat16)
-            picked = jnp.dot(picker, x_ref[low:high, half * klen : (half + 1) * klen], preferred_element_type=jnp.float32)
+            picked = jnp.dot(picker, held[half, low:high, :], preferred_element_type=jnp.float32)
             pack[half, owner, :, 0:klen] = picked[0:TILE].astype(jnp.bfloat16)
             pack[half, owner, :, klen : 2 * klen] = picked[TILE:main].astype(jnp.bfloat16)
             left = picked[main:]
@@ -141,6 +159,9 @@
     pack_half(0)
     for step in steps:
         to_owner(0, step).start()
+
+    for copy in small:
+        copy.wait()
 
     taps = taps_ref[...].astype(jnp.float32)
     square = (LANES, LANES)
@@ -194,8 +215,6 @@
     turned = jnp.transpose(matched)[0:height]
     cross[...] = jnp.zeros(cross.shape, cross.dtype)
     cross[0 : sig * crystals, 0:sig] = cross_ref[...].astype(jnp.float32).reshape(sig * crystals, sig)
-    for crystal in range(crystals):
-        coupling[crystal] = cross[pl.ds(crystal, slot, stride=crystals), :]
     lane = iota((height, depth), 1)
     part_of = jnp.where(lane < owners * main, -1, lane & (TILE - 1))
     for group in range(groups):
@@ -235,25 +254,7 @@
     place(0, 0)
     ordered[blocks] = jnp.zeros(ordered.shape[1:], ordered.dtype)
 
-    for step in steps:
-        to_owner(1, step).wait_send()
-        to_owner(0, step).wait_send()
-
-    @pl.when(later)
-    def _():
-        for step in range(owners):
-            onward(step).wait_send()
-
-
-def build_kernel(
-    sig, ordered, table, coupling, starts_ref, counts_ref, out_ref, rows_of, built, out_sem
-):
-    me = lax.axis_index("chan")
-    crystals, slot = coupling.shape[0], coupling.shape[1]
-    filters = table.shape[1] // LANES
-    half_blocks = table.shape[0] // LANES - 1
-    klen = half_blocks * LANES
-
+    filters = taps.shape[0]
     window_blocks = (SEGLEN + klen) // LANES
     seg_blocks = SEGLEN // LANES
     steps_back = half_blocks + 1
@@ -304,7 +305,7 @@
                 ],
                 axis=1,
             ).astype(jnp.bfloat16)
-            mixer = coupling[at][:, 0:slot].astype(jnp.bfloat16)
+            mixer = cross[pl.ds(at, slot, stride=crystals), :][:, 0:slot].astype(jnp.bfloat16)
             coupled = pieces.astype(jnp.float32) + jnp.dot(
                 mixer, pieces, preferred_element_type=jnp.float32
             )
@@ -322,6 +323,14 @@
                     ] = jnp.where(live, fitted, 0.0)
             built[at] = rows_of[at, 0 : built.shape[1], :].astype(built.dtype)
             pltpu.make_async_copy(built.at[at], out_ref.at[at], out_sem.at[at]).start()
+    for step in steps:
+        to_owner(1, step).wait_send()
+        to_owner(0, step).wait_send()
+
+    @pl.when(later)
+    def _():
+        for step in range(owners):
+            onward(step).wait_send()
     for at in range(crystals):
         pltpu.make_async_copy(built.at[at], out_ref.at[at], out_sem.at[at]).wait()
 
@@ -337,46 +346,46 @@
     height = crystals * slot
     packed = 2 * klen + GROUP
     blocks = SEGLEN // LANES
-    in_vmem = pl.BlockSpec(memory_space=pltpu.VMEM)
     in_smem = pl.BlockSpec(memory_space=pltpu.SMEM)
     in_hbm = pl.BlockSpec(memory_space=pltpu.HBM)
-    ordered, table, coupling = pl.pallas_call(
-        functools.partial(gather_kernel, owners, shards),
-        out_shape=(
-            jax.ShapeDtypeStruct(((samples + klen) // LANES + 1, height, LANES), jnp.float32),
-            jax.ShapeDtypeStruct((klen + LANES, filters * LANES), jnp.bfloat16),
-            jax.ShapeDtypeStruct((crystals, slot, LANES), jnp.float32),
-        ),
-        in_specs=[in_vmem] * 4,
-        out_specs=(in_vmem,) * 3,
+    built = pl.pallas_call(
+        functools.partial(kernel, owners, shards),
+        out_shape=jax.ShapeDtypeStruct((crystals, sig * blocks * filters, LANES), jnp.bfloat16),
+        in_specs=[in_hbm] * 4 + [in_smem] * 2,
+        out_specs=in_hbm,
         scratch_shapes=[
+            pltpu.VMEM((2, rows, klen), jnp.bfloat16),
+            pltpu.VMEM(kernels.shape, kernels.dtype),
+            pltpu.VMEM(chan_map.shape, chan_map.dtype),
+            pltpu.VMEM((sig, crystals, sig), crosstalk.dtype),
             pltpu.VMEM((2, owners, TILE, packed), jnp.bfloat16),
             pltpu.VMEM((3, owners, TILE, packed), jnp.bfloat16),
             pltpu.VMEM((TILE // (sig - 2 * TILE), height, owners * 3 * TILE), jnp.bfloat16),
+            pltpu.VMEM(((samples + klen) // LANES + 1, height, LANES), jnp.float32),
             pltpu.VMEM((height, LANES), jnp.float32),
+            pltpu.VMEM((klen + LANES, filters * LANES), jnp.bfloat16),
+            pltpu.VMEM((crystals, slot * blocks * filters, LANES), jnp.float32),
+            pltpu.VMEM((crystals, sig * blocks * filters, LANES), jnp.bfloat16),
+            pltpu.SemaphoreType.DMA((2,)),
+            pltpu.SemaphoreType.DMA((3,)),
             pltpu.SemaphoreType.DMA((2, owners)),
             pltpu.SemaphoreType.DMA((2, owners)),
             pltpu.SemaphoreType.DMA((owners,)),
             pltpu.SemaphoreType.DMA((owners,)),
+            pltpu.SemaphoreType.DMA((crystals,)),
         ],
         compiler_params=pltpu.CompilerParams(
-            collective_id=0, has_side_effects=True, vmem_limit_bytes=32 * 1024 * 1024
+            collective_id=0, has_side_effects=True, vmem_limit_bytes=62 * 1024 * 1024
         ),
-        name="gather_rows",
-    )(signals, kernels, chan_map, jnp.transpose(crosstalk, (1, 0, 2)))
-    built = pl.pallas_call(
-        functools.partial(build_kernel, sig),
-        out_shape=jax.ShapeDtypeStruct((crystals, sig * blocks * filters, LANES), jnp.bfloat16),
-        in_specs=[in_vmem] * 3 + [in_smem] * 2,
-        out_specs=in_hbm,
-        scratch_shapes=[
-            pltpu.VMEM((crystals, slot * blocks * filters, LANES), jnp.float32),
-            pltpu.VMEM((crystals, sig * blocks * filters, LANES), jnp.bfloat16),
-            pltpu.SemaphoreType.DMA((crystals,)),
-        ],
-        compiler_params=pltpu.CompilerParams(vmem_limit_bytes=32 * 1024 * 1024),
         name="build_events",
-    )(ordered, table, coupling, starts.reshape(-1), counts.reshape(-1))
+    )(
+        signals,
+        kernels,
+        chan_map,
+        jnp.transpose(crosstalk, (1, 0, 2)),
+        starts.reshape(-1),
+        counts.reshape(-1),
+    )
     parts = built.reshape(crystals, sig, blocks, filters, LANES)
     return jnp.transpose(parts, (0, 3, 1, 2, 4)).reshape(crystals, 1, slots, filters, sig, SEGLEN)
 

time: 23.2 us -> 21 us (0.905)
  local copies, waits for them, and re-layouts: 4.7 us -> 2.31 us
  Pallas kernels: 18.1 us -> 18.6 us
    unnamed x12 -> x1, local copies, waits for them, and re-layouts: 4.7 us -> 2.31 us
    pallas_call x2 -> x1, Pallas kernels: 18.1 us -> 18.6 us  [body(): pl.pallas_call(functools.partial(kernel, owners, shards), out_shape=jax.S...]
where the time goes in v4:
time: 21 us; the launch traced here: 20.9 us
  Pallas kernels  18.6 us (89%)
  local copies, waits for them, and re-layouts  2.31 us (11%)
    pallas_call x1, Pallas kernels, body(): pl.pallas_call(functools.partial(kernel, owners, shards), out_shape=jax.S...  18.6 us
    unnamed x1, local copies, waits for them, and re-layouts  2.31 us

profile of v4, /device:TPU:1, one launch (start us, length us, event | category | flops | bytes accessed | tf_op | source)
XLA Modules:
  0.0 20.9 jit_solution(11105238905591202506)
XLA Ops:
  0.0 18.6 %build_events.1 = bf16[8,296,128]{2,1,0:T(8,128)(2,1)} custom-call(bf16[296,1280]{1,0:T(8,128)(2,1)} %x_ref.1, bf16[2,640]{1,0:T(2,128)(2,1)} %taps_hbm.1, s32[2368]{0:T(1024)} %map_hbm.1, bf16[37,8,37]{2,1,0:T(8,128)(2,1)} %bitcast.9, s32[64]{0:T(128)} %bitcast.10, s32[64]{0:T(128)} %bitcast.11), custom_call_target="tpu_custom_call" | custom-call | tf_op jit(solution)/shard_map/build_events/pallas_call | solution.py:351
  18.6 2.3 %copy.9 = bf16[8,1,1,2,37,512]{5,3,4,2,1,0:T(2,128)(2,1)} copy(bf16[8,1,1,2,37,512]{5,3,4,2,1,0:T(2,128)(2,1)} %bitcast.8) | data formatting | bytes 1212416

commit v5 on v3

--- a/solution.py
+++ b/solution.py
@@ -13,6 +13,7 @@
 TILE = 16
 GROUP = 256
 SLOT_ROWS = 8
+VMEM_BYTES = 56 * 1024 * 1024
 MESH = pl.DeviceIdType.MESH
 
 
@@ -25,8 +26,10 @@
 
 
 def gather_kernel(
-    owners, shards, x_ref, taps_ref, map_ref, cross_ref, ordered, table, coupling,
-    pack, arrived, placer, cross, chan_send, chan_recv, tail_send, tail_recv,
+    owners, shards, x_ref, taps_hbm, map_hbm, cross_hbm, starts_ref, counts_ref,
+    ordered, table, coupling, plan,
+    held, taps_ref, map_ref, cross_ref, pack, arrived, placer, cross,
+    load_sem, small_sem, chan_send, chan_recv, tail_send, tail_recv,
 ):
     me = lax.axis_index("chan")
     shard = lax.axis_index("tm")
@@ -42,6 +45,22 @@
     half_blocks = klen // LANES
     later = shard < shards - 1
 
+    def load(half):
+        return pltpu.make_async_copy(
+            x_ref.at[:, half * klen : (half + 1) * klen], held.at[half], load_sem.at[half]
+        )
+
+    small = [
+        pltpu.make_async_copy(source, target, small_sem.at[at])
+        for at, (source, target) in enumerate(
+            [(taps_hbm, taps_ref), (map_hbm, map_ref), (cross_hbm, cross_ref)]
+        )
+    ]
+    load(1).start()
+    load(0).start()
+    for copy in small:
+        copy.start()
+
     def partner(step):
         if owners & (owners - 1) == 0:
             return me ^ step, me ^ step
@@ -67,6 +86,7 @@
         return jnp.where(index < main, index, main + turned)
 
     def pack_half(half):
+        load(half).wait()
         for owner in range(owners):
             base = owner * sig
             low = base // TILE * TILE
@@ -76,7 +96,7 @@
             wanted = base + rest_row(index)
             hit = jnp.logical_and(iota(shape, 1) + low == wanted, index < main + groups * rest)
             picker = jnp.where(hit, 1.0, 0.0).astype(jnp.bfloat16)
-            picked = jnp.dot(picker, x_ref[low:high, half * klen : (half + 1) * klen], preferred_element_type=jnp.float32)
+            picked = jnp.dot(picker, held[half, low:high, :], preferred_element_type=jnp.float32)
             pack[half, owner, :, 0:klen] = picked[0:TILE].astype(jnp.bfloat16)
             pack[half, owner, :, klen : 2 * klen] = picked[TILE:main].astype(jnp.bfloat16)
             left = picked[main:]
@@ -141,6 +161,9 @@
     pack_half(0)
     for step in steps:
         to_owner(0, step).start()
+
+    for copy in small:
+        copy.wait()
 
     taps = taps_ref[...].astype(jnp.float32)
     square = (LANES, LANES)
@@ -192,6 +215,15 @@
     wanted = jnp.where(signal_of < sig, crystal_of * sig + signal_of + me * rows + 1, -1)
     matched = jnp.where(column == wanted.astype(jnp.float32), 1.0, 0.0)
     turned = jnp.transpose(matched)[0:height]
+    lane = iota((1, LANES), 1)
+    begins = jnp.zeros((1, LANES), jnp.int32)
+    lives = jnp.zeros((1, LANES), jnp.int32)
+    for crystal in range(crystals):
+        begins = jnp.where(lane == crystal, starts_ref[me * crystals + crystal], begins)
+        lives = jnp.where(lane == crystal, counts_ref[me * crystals + crystal], lives)
+    plan[0:1] = begins
+    plan[1:2] = lives
+
     cross[...] = jnp.zeros(cross.shape, cross.dtype)
     cross[0 : sig * crystals, 0:sig] = cross_ref[...].astype(jnp.float32).reshape(sig * crystals, sig)
     for crystal in range(crystals):
@@ -246,9 +278,8 @@
 
 
 def build_kernel(
-    sig, ordered, table, coupling, starts_ref, counts_ref, out_ref, rows_of, built, out_sem
+    sig, ordered, table, coupling, plan, out_ref, rows_of, built, out_sem
 ):
-    me = lax.axis_index("chan")
     crystals, slot = coupling.shape[0], coupling.shape[1]
     filters = table.shape[1] // LANES
     half_blocks = table.shape[0] // LANES - 1
@@ -271,7 +302,7 @@
     for crystal in range(0, crystals, pair):
         windows = []
         for member in range(crystal, crystal + pair):
-            start = starts_ref[me * crystals + member]
+            start = plan[0, member]
             first = start >> 7
             shift = start & (LANES - 1)
             back = (LANES - shift) & (LANES - 1)
@@ -296,7 +327,7 @@
         filtered = jnp.dot(wide, taps_table, preferred_element_type=jnp.float32)
         for member in range(pair):
             at = crystal + member
-            live = counts_ref[me * crystals + at] > 0
+            live = plan[1, at] > 0
             pieces = jnp.concatenate(
                 [
                     filtered[b * high + member * slot : b * high + (member + 1) * slot]
@@ -340,43 +371,57 @@
     in_vmem = pl.BlockSpec(memory_space=pltpu.VMEM)
     in_smem = pl.BlockSpec(memory_space=pltpu.SMEM)
     in_hbm = pl.BlockSpec(memory_space=pltpu.HBM)
-    ordered, table, coupling = pl.pallas_call(
+    ordered, table, coupling, plan = pl.pallas_call(
         functools.partial(gather_kernel, owners, shards),
         out_shape=(
-            jax.ShapeDtypeStruct(((samples + klen) // LANES + 1, height, LANES), jnp.float32),
-            jax.ShapeDtypeStruct((klen + LANES, filters * LANES), jnp.bfloat16),
-            jax.ShapeDtypeStruct((crystals, slot, LANES), jnp.float32),
+            pltpu.VMEM(((samples + klen) // LANES + 1, height, LANES), jnp.float32),
+            pltpu.VMEM((klen + LANES, filters * LANES), jnp.bfloat16),
+            pltpu.VMEM((crystals, slot, LANES), jnp.float32),
+            pltpu.VMEM((2, LANES), jnp.int32),
         ),
-        in_specs=[in_vmem] * 4,
-        out_specs=(in_vmem,) * 3,
+        in_specs=[in_hbm] * 4 + [in_smem] * 2,
+        out_specs=(in_vmem,) * 4,
         scratch_shapes=[
+            pltpu.VMEM((2, rows, klen), jnp.bfloat16),
+            pltpu.VMEM(kernels.shape, kernels.dtype),
+            pltpu.VMEM(chan_map.shape, chan_map.dtype),
+            pltpu.VMEM((sig, crystals, sig), crosstalk.dtype),
             pltpu.VMEM((2, owners, TILE, packed), jnp.bfloat16),
             pltpu.VMEM((3, owners, TILE, packed), jnp.bfloat16),
             pltpu.VMEM((TILE // (sig - 2 * TILE), height, owners * 3 * TILE), jnp.bfloat16),
             pltpu.VMEM((height, LANES), jnp.float32),
+            pltpu.SemaphoreType.DMA((2,)),
+            pltpu.SemaphoreType.DMA((3,)),
             pltpu.SemaphoreType.DMA((2, owners)),
             pltpu.SemaphoreType.DMA((2, owners)),
             pltpu.SemaphoreType.DMA((owners,)),
             pltpu.SemaphoreType.DMA((owners,)),
         ],
         compiler_params=pltpu.CompilerParams(
-            collective_id=0, has_side_effects=True, vmem_limit_bytes=32 * 1024 * 1024
+            collective_id=0, has_side_effects=True, vmem_limit_bytes=VMEM_BYTES
         ),
         name="gather_rows",
-    )(signals, kernels, chan_map, jnp.transpose(crosstalk, (1, 0, 2)))
+    )(
+        signals,
+        kernels,
+        chan_map,
+        jnp.transpose(crosstalk, (1, 0, 2)),
+        starts.reshape(-1),
+        counts.reshape(-1),
+    )
     built = pl.pallas_call(
         functools.partial(build_kernel, sig),
         out_shape=jax.ShapeDtypeStruct((crystals, sig * blocks * filters, LANES), jnp.bfloat16),
-        in_specs=[in_vmem] * 3 + [in_smem] * 2,
+        in_specs=[in_vmem] * 3 + [in_smem],
         out_specs=in_hbm,
         scratch_shapes=[
             pltpu.VMEM((crystals, slot * blocks * filters, LANES), jnp.float32),
             pltpu.VMEM((crystals, sig * blocks * filters, LANES), jnp.bfloat16),
             pltpu.SemaphoreType.DMA((crystals,)),
         ],
-        compiler_params=pltpu.CompilerParams(vmem_limit_bytes=32 * 1024 * 1024),
+        compiler_params=pltpu.CompilerParams(vmem_limit_bytes=24 * 1024 * 1024),
         name="build_events",
-    )(ordered, table, coupling, starts.reshape(-1), counts.reshape(-1))
+    )(ordered, table, coupling, plan)
     parts = built.reshape(crystals, sig, blocks, filters, LANES)
     return jnp.transpose(parts, (0, 3, 1, 2, 4)).reshape(crystals, 1, slots, filters, sig, SEGLEN)
 

time: 23.2 us -> 19.1 us (0.82)
  local copies, waits for them, and re-layouts: 4.7 us -> 0 us
  Pallas kernels: 18.1 us -> 18.9 us
    unnamed x12 -> x0, local copies, waits for them, and re-layouts: 4.7 us -> none
    pallas_call x1, Pallas kernels: 15 us -> 15.8 us  [body(): pl.pallas_call(functools.partial(gather_kernel, owners, shards), out_shap...]
where the time goes in v5:
time: 19.1 us; the launch traced here: 18.9 us
  Pallas kernels  18.9 us (99%)
    pallas_call x1, Pallas kernels, body(): pl.pallas_call(functools.partial(gather_kernel, owners, shards), out_shap...  15.8 us
    pallas_call x1, Pallas kernels, body(): pl.pallas_call(functools.partial(build_kernel, sig), out_shape=jax.ShapeD...  3.17 us

profile of v5, /device:TPU:1, one launch (start us, length us, event | category | flops | bytes accessed | tf_op | source)
XLA Modules:
  0.0 18.9 jit_solution(864565718286470419)
XLA Ops:
  0.0 15.8 %gather_rows.1 = (f32[16,320,128]{2,1,0:T(8,128)S(1)}, bf16[768,256]{1,0:T(8,128)(2,1)S(1)}, f32[8,40,128]{2,1,0:T(8,128)S(1)}, s32[2,128]{1,0:T(2,128)S(1)}) custom-call(bf16[296,1280]{1,0:T(8,128)(2,1)} %x_ref.1, bf16[2,640]{1,0:T(2,128)(2,1)} %taps_hbm.1, s32[2368]{0:T(1024)} %map_hbm.1, bf16[37,8,37]{2,1,0:T(8,128)(2,1)} %bitcast.8, s32[64]{0:T(128)} %bitcast.9, ...), custom_call_target="tpu_custom_call" | custom-call | tf_op jit(solution)/shard_map/gather_rows/pallas_call | solution.py:374
  15.8 3.2 %build_events.1 = bf16[8,296,128]{2,1,0:T(8,128)(2,1)} custom-call(f32[16,320,128]{2,1,0:T(8,128)S(1)} %get-tuple-element.9.ordered, bf16[768,256]{1,0:T(8,128)(2,1)S(1)} %get-tuple-element.10.table, f32[8,40,128]{2,1,0:T(8,128)S(1)} %get-tuple-element.11.coupling, s32[2,128]{1,0:T(2,128)S(1)} %get-tuple-element.12.plan), custom_call_target="tpu_custom_call" | custom-call | tf_op jit(solution)/shard_map/build_events/pallas_call | solution.py:412

commit v6 on v5

--- a/solution.py
+++ b/solution.py
@@ -28,7 +28,7 @@
 def gather_kernel(
     owners, shards, x_ref, taps_hbm, map_hbm, cross_hbm, starts_ref, counts_ref,
     ordered, table, coupling, plan,
-    held, taps_ref, map_ref, cross_ref, pack, arrived, placer, cross,
+    held, taps_ref, map_ref, cross_ref, pack, arrived, placer, slots_ref, cross,
     load_sem, small_sem, chan_send, chan_recv, tail_send, tail_recv,
 ):
     me = lax.axis_index("chan")
@@ -68,6 +68,11 @@
 
     steps = [step for low in range(2) for step in range(low, owners, 2)]
     steps = [1] + [step for step in steps if step > 1] if owners > 1 else []
+    place_of = {step: at for at, step in enumerate([0] + steps)}
+    splits = 2
+    share = owners // splits
+    span = share * (main + TILE)
+    depth = round_up(span, LANES)
 
     barrier = pltpu.get_barrier_semaphore()
     for step in range(1, owners):
@@ -108,7 +113,7 @@
                 jnp.where(row < 2 * rest, left[:, GROUP : 2 * GROUP], jnp.concatenate([last, last], axis=1)),
             )
             pack[half, owner, :, 2 * klen : 2 * klen + GROUP] = kept.astype(jnp.bfloat16)
-        arrived[half + 1, me] = pack[half, me]
+        arrived[half + 1, 0] = pack[half, me]
 
     pack_half(1)
 
@@ -122,7 +127,7 @@
         peer = partner(step)[0]
         return pltpu.make_async_remote_copy(
             src_ref=pack.at[half, peer],
-            dst_ref=arrived.at[half + 1, me],
+            dst_ref=arrived.at[half + 1, place_of[step]],
             send_sem=chan_send.at[half, step],
             recv_sem=chan_recv.at[half, step],
             device_id={"chan": peer},
@@ -133,7 +138,7 @@
         peer = partner(step)[1]
         return pltpu.make_async_remote_copy(
             src_ref=pack.at[half, peer],
-            dst_ref=arrived.at[half + 1, peer],
+            dst_ref=arrived.at[half + 1, place_of[step]],
             send_sem=chan_send.at[half, step],
             recv_sem=chan_recv.at[half, step],
             device_id={"chan": peer},
@@ -141,10 +146,9 @@
         )
 
     def onward(step):
-        peer = partner(step)[1] if step else me
         return pltpu.make_async_remote_copy(
-            src_ref=arrived.at[2, peer],
-            dst_ref=arrived.at[0, peer],
+            src_ref=arrived.at[2, place_of[step]],
+            dst_ref=arrived.at[0, place_of[step]],
             send_sem=tail_send.at[step],
             recv_sem=tail_recv.at[step],
             device_id={"tm": jnp.minimum(shard + 1, shards - 1)},
@@ -190,7 +194,7 @@
         def _():
             onward(step).start()
 
-    columns = []
+    slots_ref[...] = jnp.full(slots_ref.shape, -5.0, slots_ref.dtype)
     total = map_ref.shape[0]
     for source in range(owners):
         low = source * rows // LANES * LANES
@@ -200,12 +204,17 @@
         wanted = source * rows + me * sig + rest_row(index)
         hit = jnp.logical_and(iota(shape, 1) + low == wanted, index < main + groups * rest)
         names = (map_ref[low:high].astype(jnp.float32) + 1.0).reshape(1, high - low)
-        columns.append(jnp.sum(jnp.where(hit, names, 0.0), axis=1, keepdims=True))
-    column = jnp.concatenate(
-        [c[0:TILE] for c in columns] + [c[TILE:main] for c in columns] + [c[main:] for c in columns],
-        axis=0,
-    )
-    depth = owners * (main + TILE)
+        column = jnp.sum(jnp.where(hit, names, 0.0), axis=1, keepdims=True)
+        column = jnp.broadcast_to(column, (main + TILE, LANES))
+        step_to = me ^ source if owners & (owners - 1) == 0 else lax.rem(me - source + owners, owners)
+        at = 0
+        for step, place_at in place_of.items():
+            first = place_at // share * depth + place_at % share * TILE
+            at = at + jnp.where(step_to == step, first, 0)
+        for part in range(3):
+            target = pl.ds(pl.multiple_of(at + part * share * TILE, TILE), TILE)
+            slots_ref[target, :] = column[part * TILE : (part + 1) * TILE]
+    column = slots_ref[:, 0:1]
     width = round_up(height, LANES)
     lane = iota((1, width), 1)
     crystal_of = jnp.zeros((1, width), jnp.int32)
@@ -229,14 +238,17 @@
     for crystal in range(crystals):
         coupling[crystal] = cross[pl.ds(crystal, slot, stride=crystals), :]
     lane = iota((height, depth), 1)
-    part_of = jnp.where(lane < owners * main, -1, lane & (TILE - 1))
+    part_of = jnp.where(lane < share * main, -1, lane & (TILE - 1))
     for group in range(groups):
         own = jnp.logical_and(part_of >= group * rest, part_of < (group + 1) * rest)
         keep = jnp.logical_or(part_of < 0, own)
-        placer[group] = jnp.where(keep, turned, 0.0).astype(placer.dtype)
-
-    def place(part, first_block):
-        source = arrived[part].reshape(owners * TILE, arrived.shape[3])
+        for split in range(splits):
+            own = turned[:, split * depth : (split + 1) * depth]
+            placer[split, group] = jnp.where(keep, own, 0.0).astype(placer.dtype)
+
+    def place(part, first_block, split):
+        source = arrived[part, split * share : (split + 1) * share]
+        source = source.reshape(share * TILE, arrived.shape[3])
         for group in range(groups):
             low = group * GROUP
             high = min(low + GROUP, klen)
@@ -248,23 +260,28 @@
                 ],
                 axis=0,
             )
-            rows_out = jnp.dot(placer[group], stacked, preferred_element_type=jnp.float32)
+            rows_out = jnp.dot(
+                placer[split, group][:, 0:span], stacked, preferred_element_type=jnp.float32)
             for block in range((high - low) // LANES):
-                ordered[first_block + low // LANES + block] = rows_out[
-                    :, block * LANES : (block + 1) * LANES
-                ]
-
-    place(2, 2 * half_blocks)
-    for step in steps:
-        from_owner(0, step).wait_recv()
-    place(1, half_blocks)
-
-    @pl.when(shard > 0)
-    def _():
-        for step in range(owners):
-            onward(step).wait_recv()
-
-    place(0, 0)
+                at = first_block + low // LANES + block
+                piece = rows_out[:, block * LANES : (block + 1) * LANES]
+                ordered[at] = piece if split == 0 else ordered[at] + piece
+
+    members = [[step for step in place_of if place_of[step] // share == split] for split in range(splits)]
+    for split in range(splits):
+        place(2, 2 * half_blocks, split)
+    for split in range(splits):
+        for step in members[split]:
+            if step:
+                from_owner(0, step).wait_recv()
+        place(1, half_blocks, split)
+
+        @pl.when(shard > 0)
+        def _():
+            for step in members[split]:
+                onward(step).wait_recv()
+
+        place(0, 0, split)
     ordered[blocks] = jnp.zeros(ordered.shape[1:], ordered.dtype)
 
     for step in steps:
@@ -297,7 +314,7 @@
     pre_axis = fit_axis[0]
     power = jnp.sum(pre_axis * pre_axis)
     taps_table = table[...]
-    pair = 2 if crystals % 2 == 0 else 1
+    pair = 4 if crystals % 4 == 0 else 1
     high = pair * slot
     for crystal in range(0, crystals, pair):
         windows = []
@@ -351,7 +368,9 @@
                     rows_of[
                         at, pl.ds(b * filters + filter_index, slot, stride=filters * seg_blocks), :
                     ] = jnp.where(live, fitted, 0.0)
+        for at in range(crystal, crystal + pair):
             built[at] = rows_of[at, 0 : built.shape[1], :].astype(built.dtype)
+        for at in range(crystal, crystal + pair):
             pltpu.make_async_copy(built.at[at], out_ref.at[at], out_sem.at[at]).start()
     for at in range(crystals):
         pltpu.make_async_copy(built.at[at], out_ref.at[at], out_sem.at[at]).wait()
@@ -367,6 +386,7 @@
     slot = round_up(sig, SLOT_ROWS)
     height = crystals * slot
     packed = 2 * klen + GROUP
+    depth = round_up(owners // 2 * 3 * TILE, LANES)
     blocks = SEGLEN // LANES
     in_vmem = pl.BlockSpec(memory_space=pltpu.VMEM)
     in_smem = pl.BlockSpec(memory_space=pltpu.SMEM)
@@ -388,7 +408,8 @@
             pltpu.VMEM((sig, crystals, sig), crosstalk.dtype),
             pltpu.VMEM((2, owners, TILE, packed), jnp.bfloat16),
             pltpu.VMEM((3, owners, TILE, packed), jnp.bfloat16),
-            pltpu.VMEM((TILE // (sig - 2 * TILE), height, owners * 3 * TILE), jnp.bfloat16),
+            pltpu.VMEM((2, TILE // (sig - 2 * TILE), height, depth), jnp.bfloat16),
+            pltpu.VMEM((2 * depth, LANES), jnp.float32),
             pltpu.VMEM((height, LANES), jnp.float32),
             pltpu.SemaphoreType.DMA((2,)),
             pltpu.SemaphoreType.DMA((3,)),

time: 19.1 us -> 19 us (level)
  no operation moved by 1% of the time
where the time goes in v6:
time: 19 us; the launch traced here: 18.8 us
  Pallas kernels  18.8 us (99%)
    pallas_call x1, Pallas kernels, body(): pl.pallas_call(functools.partial(gather_kernel, owners, shards), out_shap...  15.6 us
    pallas_call x1, Pallas kernels, body(): pl.pallas_call(functools.partial(build_kernel, sig), out_shape=jax.ShapeD...  3.24 us

profile of v6, /device:TPU:1, one launch (start us, length us, event | category | flops | bytes accessed | tf_op | source)
XLA Modules:
  0.0 18.8 jit_solution(8577609906823648616)
XLA Ops:
  0.0 15.6 %gather_rows.1 = (f32[16,320,128]{2,1,0:T(8,128)S(1)}, bf16[768,256]{1,0:T(8,128)(2,1)S(1)}, f32[8,40,128]{2,1,0:T(8,128)S(1)}, s32[2,128]{1,0:T(2,128)S(1)}) custom-call(bf16[296,1280]{1,0:T(8,128)(2,1)} %x_ref.1, bf16[2,640]{1,0:T(2,128)(2,1)} %taps_hbm.1, s32[2368]{0:T(1024)} %map_hbm.1, bf16[37,8,37]{2,1,0:T(8,128)(2,1)} %bitcast.8, s32[64]{0:T(128)} %bitcast.9, ...), custom_call_target="tpu_custom_call" | custom-call | tf_op jit(solution)/shard_map/gather_rows/pallas_call | solution.py:394
  15.6 3.2 %build_events.1 = bf16[8,296,128]{2,1,0:T(8,128)(2,1)} custom-call(f32[16,320,128]{2,1,0:T(8,128)S(1)} %get-tuple-element.9.ordered, bf16[768,256]{1,0:T(8,128)(2,1)S(1)} %get-tuple-element.10.table, f32[8,40,128]{2,1,0:T(8,128)S(1)} %get-tuple-element.11.coupling, s32[2,128]{1,0:T(2,128)S(1)} %get-tuple-element.12.plan), custom_call_target="tpu_custom_call" | custom-call | tf_op jit(solution)/shard_map/build_events/pallas_call | solution.py:433

commit v7 on v6

--- a/solution.py
+++ b/solution.py
@@ -66,8 +66,8 @@
             return me ^ step, me ^ step
         return lax.rem(me + step, owners), lax.rem(me + owners - step, owners)
 
-    steps = [step for low in range(2) for step in range(low, owners, 2)]
-    steps = [1] + [step for step in steps if step > 1] if owners > 1 else []
+    steps = sorted(range(2, owners), key=lambda step: (-bin(step >> 1).count("1"), step & 1, step))
+    steps = [1] + steps if owners > 1 else []
     place_of = {step: at for at, step in enumerate([0] + steps)}
     splits = 2
     share = owners // splits
@@ -314,7 +314,7 @@
     pre_axis = fit_axis[0]
     power = jnp.sum(pre_axis * pre_axis)
     taps_table = table[...]
-    pair = 4 if crystals % 4 == 0 else 1
+    pair = 2 if crystals % 2 == 0 else 1
     high = pair * slot
     for crystal in range(0, crystals, pair):
         windows = []

time: 19 us -> 19.5 us (1.026)
  the two profiles are of different devices: /device:TPU:1 before, /device:TPU:0 now
where the time goes in v7:
time: 19.5 us; the launch traced here: 19.4 us
  Pallas kernels  19.4 us (99%)
    pallas_call x1, Pallas kernels, body(): pl.pallas_call(functools.partial(gather_kernel, owners, shards), out_shap...  16.2 us
    pallas_call x1, Pallas kernels, body(): pl.pallas_call(functools.partial(build_kernel, sig), out_shape=jax.ShapeD...  3.19 us

profile of v7, /device:TPU:0, one launch (start us, length us, event | category | flops | bytes accessed | tf_op | source)
XLA Modules:
  0.0 19.4 jit_solution(8083557777102492743)
XLA Ops:
  0.0 16.2 %gather_rows.1 = (f32[16,320,128]{2,1,0:T(8,128)S(1)}, bf16[768,256]{1,0:T(8,128)(2,1)S(1)}, f32[8,40,128]{2,1,0:T(8,128)S(1)}, s32[2,128]{1,0:T(2,128)S(1)}) custom-call(bf16[296,1280]{1,0:T(8,128)(2,1)} %x_ref.1, bf16[2,640]{1,0:T(2,128)(2,1)} %taps_hbm.1, s32[2368]{0:T(1024)} %map_hbm.1, bf16[37,8,37]{2,1,0:T(8,128)(2,1)} %bitcast.8, s32[64]{0:T(128)} %bitcast.9, ...), custom_call_target="tpu_custom_call" | custom-call | tf_op jit(solution)/shard_map/gather_rows/pallas_call | solution.py:394
  16.2 3.2 %build_events.1 = bf16[8,296,128]{2,1,0:T(8,128)(2,1)} custom-call(f32[16,320,128]{2,1,0:T(8,128)S(1)} %get-tuple-element.9.ordered, bf16[768,256]{1,0:T(8,128)(2,1)S(1)} %get-tuple-element.10.table, f32[8,40,128]{2,1,0:T(8,128)S(1)} %get-tuple-element.11.coupling, s32[2,128]{1,0:T(2,128)S(1)} %get-tuple-element.12.plan), custom_call_target="tpu_custom_call" | custom-call | tf_op jit(solution)/shard_map/build_events/pallas_call | solution.py:433
